TPU v7x, 512 devices: a whole 4x4x16 slice. The times are simulated.
512 devices in a mesh: dp: 2 (over y_hi), ctx: 32 (over z, y_lo), tp: 8 (over x, core).
Axes of the slice: x: 4, y: 4 (y_hi: 2, y_lo: 2; y = y_hi * 2 + y_lo), z: 16, core: 2. Of those that a mesh axis runs over, the one named last changes fastest.
Arguments:
- queries: bfloat16 [16384, 8192], P(('dp', 'ctx'), 'tp'), parts along dimension 0
- keys: bfloat16 [16384, 1024], P(('dp', 'ctx'), 'tp'), parts along dimension 0
- values: bfloat16 [16384, 1024], P(('dp', 'ctx'), 'tp'), parts along dimension 0, may hold values from -6 to 6
- query_norm_gain: float32 [128], replicated, may hold values from 0.1 to 1.9
- key_norm_gain: float32 [128], replicated, may hold values from 0.1 to 1.9
- positions: int32 [16384], P(('dp', 'ctx')), parts along dimension 0, may hold values from 0 to 4607, as said below
- segment_ids: int32 [16384], P(('dp', 'ctx')), parts along dimension 0, may hold values from 0 to 16, as said below
- block_mask: int32 [128, 64], P(('dp', 'ctx')), parts along dimension 0, may hold values from 0 to 1, as said below
Outputs:
- attended: bfloat16 [16384, 8192], P(('dp', 'ctx'), 'tp'), parts along dimension 0
There are 2 independent parts, one for each index of `dp`. A program takes and returns all parts, laid end to end along the dimension named above; an argument that names none is the same for every part. Nothing has to cross between parts.
Inputs may be any that keep to these rules, and one draw needn't show every extreme that they name: segment_ids is 0 on the first 4096 tokens; then the responses 1 to 16 follow in order, each one contiguous run of 1 to 512 tokens, one of exactly 512, the last ending at the pack's end. `positions`: a prompt token's position is its index; a response token's is 4096 plus its offset in its response. block_mask[a, b] is 1 exactly when some token of block a may see some token of block b under the token rule, else 0.
All inputs are finite; a program needn't handle non-finite values.
Results may differ from a plain program's by a relative error of at most 0.0073.
Values may be sent and summed in bfloat16 or wider, within the bound.
No kernel may reach another device: no remote copies, remote signals or barrier semaphores. Data moves between devices by JAX's collectives and lax.ppermute only.
A program may use at most 64 MiB of HBM per device.

v0:
```python
import math

import jax
import jax.numpy as jnp
from jax import lax
from jax.sharding import PartitionSpec as P


def apply_rotary_embedding(source, gain, positions, heads):
    count = source.shape[0]
    size = gain.shape[0]
    vec = source.astype(jnp.float32).reshape(count, heads, size)
    vec = vec * lax.rsqrt(jnp.mean(vec * vec, axis=-1, keepdims=True) + 1e-06) * gain
    half = size // 2
    freq = jnp.exp(-math.log(1000000.0) * jnp.arange(half, dtype=jnp.float32) * (2.0 / size))
    angle = positions.astype(jnp.float32)[:, None] * freq[None, :]
    cosine = jnp.cos(angle)[:, None, :]
    sine = jnp.sin(angle)[:, None, :]
    first = vec[..., :half]
    second = vec[..., half:]
    out = jnp.concatenate([first * cosine - second * sine, second * cosine + first * sine], axis=-1)
    return out.astype(jnp.bfloat16)


def local(
    queries, keys, values, query_norm_gain, key_norm_gain, positions, segment_ids, block_mask
):
    rows = queries.shape[0]
    head_size = query_norm_gain.shape[0]
    kv_heads = keys.shape[1] // head_size
    per_group = queries.shape[1] // (kv_heads * head_size)
    cycle_size = lax.axis_size("ctx")
    mine = lax.axis_index("ctx")
    pack_len = cycle_size * rows
    prompt_len = pack_len // 2
    mask_block = pack_len // block_mask.shape[1]
    scale = head_size ** (-0.5)
    query_rotated_rows = apply_rotary_embedding(
        queries, query_norm_gain, positions, kv_heads * per_group
    ).reshape(rows, kv_heads, per_group, head_size)
    key_rotated_rows = apply_rotary_embedding(keys, key_norm_gain, positions, kv_heads).reshape(
        rows, kv_heads * head_size
    )
    seg_send = segment_ids.astype(jnp.bfloat16)
    qseg = segment_ids.astype(jnp.float32)
    query_index = mine * rows + jnp.arange(rows, dtype=jnp.int32)
    table_cols = jnp.repeat(block_mask, mask_block, axis=1)
    init = (
        jnp.zeros((kv_heads, per_group, rows), jnp.float32),
        jnp.zeros((kv_heads, per_group, rows, head_size), jnp.float32),
    )
    key_part = lax.all_gather(key_rotated_rows, "ctx", axis=0, tiled=True)
    value_part = lax.all_gather(values, "ctx", axis=0, tiled=True)
    seg_part = lax.all_gather(seg_send, "ctx", axis=0, tiled=True)
    count = key_part.shape[0]
    sub = math.gcd(count, 512)

    def one(step, state):
        first = step * sub
        key_blk = lax.dynamic_slice_in_dim(key_part, first, sub, 0).reshape(
            sub, kv_heads, head_size
        )
        value_blk = lax.dynamic_slice_in_dim(value_part, first, sub, 0).reshape(
            sub, kv_heads, head_size
        )
        seg_blk = lax.dynamic_slice_in_dim(seg_part, first, sub, 0).astype(jnp.float32)
        key_index = first + jnp.arange(sub, dtype=jnp.int32)
        live = lax.dynamic_slice_in_dim(table_cols, first, sub, 1)
        live = jnp.repeat(live, mask_block, axis=0)
        mask = (live > 0) & (key_index[None, :] <= query_index[:, None])
        mask = mask & ((key_index < prompt_len)[None, :] | (seg_blk[None, :] == qseg[:, None]))
        mask = mask & True

        def compute(old):
            score = (
                jnp.einsum(
                    "qkgd,jkd->kgqj",
                    query_rotated_rows,
                    key_blk,
                    preferred_element_type=jnp.float32,
                )
                * scale
            )
            weight = jnp.where(mask[None, None], jnp.exp(score), jnp.float32(0.0))
            total = old[0] + jnp.sum(weight, axis=-1)
            acc = old[1] + jnp.einsum(
                "kgqj,jkd->kgqd",
                weight.astype(jnp.bfloat16),
                value_blk,
                preferred_element_type=jnp.float32,
            )
            return (total, acc)

        return lax.cond(jnp.any(mask), compute, lambda old: old, state)

    total, acc = lax.fori_loop(0, count // sub, one, init)
    result = (acc / total[..., None]).astype(jnp.bfloat16)
    return jnp.transpose(result, (2, 0, 1, 3)).reshape(rows, kv_heads * per_group * head_size)


def solution(mesh):
    return jax.shard_map(
        local,
        mesh=mesh,
        in_specs=(
            P(("dp", "ctx"), "tp"),
            P(("dp", "ctx"), "tp"),
            P(("dp", "ctx"), "tp"),
            P(),
            P(),
            P(("dp", "ctx")),
            P(("dp", "ctx")),
            P(("dp", "ctx"), None),
        ),
        out_specs=P(("dp", "ctx"), "tp"),
        check_vma=False,
    )
```

profile of v0, /device:TPU:384, one launch (start us, length us, event | category | flops | bytes accessed | tf_op | source)
XLA Modules:
  0.0 360.6 jit_solution(17344165943293947504)
XLA Ops:
  6.5 1.0 fusion.37
  7.5 0.7 convert_element_type.51
  8.2 0.9 fusion.39
  9.1 0.6 fusion.45
  9.7 0.7 pad_maximum_fusion.1
  10.5 0.7 all-gather.6.cloned.1.call-update
  11.4 0.8 fusion.46
  12.2 61.7 %all-gather = bf16[32,1,256]{2,1,0:T(2,128)(2,1)S(1)} all-gather(bf16[1,1,256]{2,1,0:T(2,128)(2,1)S(1)} %reshape.292), channel_id=1, replica_groups=mesh['dp'=2,'ctx'=32,'tp'=8] {'ctx'}, dimensions={0}, use_global_device_ids=true | all-gather | bytes 16896 | tf_op jit(solution)/shard_map/all_gather | solution.py:54
  73.9 1.2 copy.25
  75.3 0.3 multiply_cosine_fusion.1
  75.6 0.8 fusion.29
  76.7 0.3 copy.26
  77.0 65.1 %all-gather.4.cloned.1.call-done = bf16[8192,128]{1,0:T(8,128)(2,1)} async-done(((bf16[256,128]{1,0:T(8,128)(2,1)}), bf16[8192,128]{1,0:T(8,128)(2,1)}) %all-gather.4.cloned.1.call-update) | async-done | bytes 2097168 | tf_op jit(solution)/shard_map/all_gather | solution.py:52
  142.1 134.7 %all-gather.6.cloned.1.call-done = bf16[8192,128]{1,0:T(8,128)(2,1)} async-done(((bf16[256,128]{1,0:T(8,128)(2,1)}), bf16[8192,128]{1,0:T(8,128)(2,1)}) %all-gather.6.cloned.1.call-update) | async-done | bytes 2097168 | tf_op jit(solution)/shard_map/all_gather | solution.py:53
  276.8 75.3 %while.16 = (s32[]{:T(128)}, f32[1,8,256]{2,1,0:T(8,128)S(1)}, f32[1,8,256,128]{3,2,1,0:T(8,128)S(1)}, s32[2,8192]{1,0:T(2,128)S(1)}, bf16[8192]{0:T(1024)(128)(...) while((s32[]{:T(128)}, f32[1,8,256]{2,1,0:T(8,128)S(1)}, ...), condition=%wide.region_7.8_spmd.clone, body=%wide.region_2.7_spmd.clone.sunk | while | flops 544870912 | bytes 11999073 | solution.py:96
  277.0 0.9 and_reduce_fusion.2
  278.6 4.7 %conditional.3 = ((f32[1,8,256]{2,1,0:T(8,128)S(1)}, f32[1,8,256,128]{3,2,1,0:T(8,128)S(1)})) conditional(s32[]{:T(128)} %convert_element_type.80, (f32[1,8,256]{2,1,0:T(8,128)S(1)}, f32[1,8,256,128]{3,2,1,0:T(8,128)S(1)}) %tuple.57, (s32[2,512]{1,0:T(2,128)S(1)}, s32[512]{0:T(512)S(1)}, s32[256]{0:T(256)S(1)}, pred[512]{0:T(512)(128)(4,1)S(1)}, ...), branch_computations={%region_4.0_spmd, %region_5.6_spmd} | conditional | flops 544080896 | bytes 11974168 | solution.py:94
  279.1 2.0 fusion.3
  281.1 2.2 fusion.13
  283.4 0.9 and_reduce_fusion.2
  285.0 4.7 %conditional.3 = ((f32[1,8,256]{2,1,0:T(8,128)S(1)}, f32[1,8,256,128]{3,2,1,0:T(8,128)S(1)})) conditional(s32[]{:T(128)} %convert_element_type.80, (f32[1,8,256]{2,1,0:T(8,128)S(1)}, f32[1,8,256,128]{3,2,1,0:T(8,128)S(1)}) %tuple.57, (s32[2,512]{1,0:T(2,128)S(1)}, s32[512]{0:T(512)S(1)}, s32[256]{0:T(256)S(1)}, pred[512]{0:T(512)(128)(4,1)S(1)}, ...), branch_computations={%region_4.0_spmd, %region_5.6_spmd} | conditional | flops 544080896 | bytes 11974168 | solution.py:94
  285.6 2.0 fusion.3
  287.6 2.2 fusion.13
  289.9 0.9 and_reduce_fusion.2
  291.5 4.7 %conditional.3 = ((f32[1,8,256]{2,1,0:T(8,128)S(1)}, f32[1,8,256,128]{3,2,1,0:T(8,128)S(1)})) conditional(s32[]{:T(128)} %convert_element_type.80, (f32[1,8,256]{2,1,0:T(8,128)S(1)}, f32[1,8,256,128]{3,2,1,0:T(8,128)S(1)}) %tuple.57, (s32[2,512]{1,0:T(2,128)S(1)}, s32[512]{0:T(512)S(1)}, s32[256]{0:T(256)S(1)}, pred[512]{0:T(512)(128)(4,1)S(1)}, ...), branch_computations={%region_4.0_spmd, %region_5.6_spmd} | conditional | flops 544080896 | bytes 11974168 | solution.py:94
  292.1 2.0 fusion.3
  294.1 2.2 fusion.13
  296.4 0.9 and_reduce_fusion.2
  298.0 4.7 %conditional.3 = ((f32[1,8,256]{2,1,0:T(8,128)S(1)}, f32[1,8,256,128]{3,2,1,0:T(8,128)S(1)})) conditional(s32[]{:T(128)} %convert_element_type.80, (f32[1,8,256]{2,1,0:T(8,128)S(1)}, f32[1,8,256,128]{3,2,1,0:T(8,128)S(1)}) %tuple.57, (s32[2,512]{1,0:T(2,128)S(1)}, s32[512]{0:T(512)S(1)}, s32[256]{0:T(256)S(1)}, pred[512]{0:T(512)(128)(4,1)S(1)}, ...), branch_computations={%region_4.0_spmd, %region_5.6_spmd} | conditional | flops 544080896 | bytes 11974168 | solution.py:94
  298.5 2.0 fusion.3
  300.5 2.2 fusion.13
  302.9 0.9 and_reduce_fusion.2
  304.5 4.7 %conditional.3 = ((f32[1,8,256]{2,1,0:T(8,128)S(1)}, f32[1,8,256,128]{3,2,1,0:T(8,128)S(1)})) conditional(s32[]{:T(128)} %convert_element_type.80, (f32[1,8,256]{2,1,0:T(8,128)S(1)}, f32[1,8,256,128]{3,2,1,0:T(8,128)S(1)}) %tuple.57, (s32[2,512]{1,0:T(2,128)S(1)}, s32[512]{0:T(512)S(1)}, s32[256]{0:T(256)S(1)}, pred[512]{0:T(512)(128)(4,1)S(1)}, ...), branch_computations={%region_4.0_spmd, %region_5.6_spmd} | conditional | flops 544080896 | bytes 11974168 | solution.py:94
  305.0 2.0 fusion.3
  307.0 2.2 fusion.13
  309.3 0.9 and_reduce_fusion.2
  310.9 4.7 %conditional.3 = ((f32[1,8,256]{2,1,0:T(8,128)S(1)}, f32[1,8,256,128]{3,2,1,0:T(8,128)S(1)})) conditional(s32[]{:T(128)} %convert_element_type.80, (f32[1,8,256]{2,1,0:T(8,128)S(1)}, f32[1,8,256,128]{3,2,1,0:T(8,128)S(1)}) %tuple.57, (s32[2,512]{1,0:T(2,128)S(1)}, s32[512]{0:T(512)S(1)}, s32[256]{0:T(256)S(1)}, pred[512]{0:T(512)(128)(4,1)S(1)}, ...), branch_computations={%region_4.0_spmd, %region_5.6_spmd} | conditional | flops 544080896 | bytes 11974168 | solution.py:94
  311.5 2.0 fusion.3
  313.5 2.2 fusion.13
  315.8 0.9 and_reduce_fusion.2
  317.4 4.7 %conditional.3 = ((f32[1,8,256]{2,1,0:T(8,128)S(1)}, f32[1,8,256,128]{3,2,1,0:T(8,128)S(1)})) conditional(s32[]{:T(128)} %convert_element_type.80, (f32[1,8,256]{2,1,0:T(8,128)S(1)}, f32[1,8,256,128]{3,2,1,0:T(8,128)S(1)}) %tuple.57, (s32[2,512]{1,0:T(2,128)S(1)}, s32[512]{0:T(512)S(1)}, s32[256]{0:T(256)S(1)}, pred[512]{0:T(512)(128)(4,1)S(1)}, ...), branch_computations={%region_4.0_spmd, %region_5.6_spmd} | conditional | flops 544080896 | bytes 11974168 | solution.py:94
  318.0 2.0 fusion.3
  320.0 2.2 fusion.13
  322.3 0.9 and_reduce_fusion.2
  323.9 4.7 %conditional.3 = ((f32[1,8,256]{2,1,0:T(8,128)S(1)}, f32[1,8,256,128]{3,2,1,0:T(8,128)S(1)})) conditional(s32[]{:T(128)} %convert_element_type.80, (f32[1,8,256]{2,1,0:T(8,128)S(1)}, f32[1,8,256,128]{3,2,1,0:T(8,128)S(1)}) %tuple.57, (s32[2,512]{1,0:T(2,128)S(1)}, s32[512]{0:T(512)S(1)}, s32[256]{0:T(256)S(1)}, pred[512]{0:T(512)(128)(4,1)S(1)}, ...), branch_computations={%region_4.0_spmd, %region_5.6_spmd} | conditional | flops 544080896 | bytes 11974168 | solution.py:94
  324.4 2.0 fusion.3
  326.4 2.2 fusion.13
  328.8 0.9 and_reduce_fusion.2
  330.5 0.9 and_reduce_fusion.2
  332.3 0.9 and_reduce_fusion.2
  334.1 0.9 and_reduce_fusion.2
  335.7 4.7 %conditional.3 = ((f32[1,8,256]{2,1,0:T(8,128)S(1)}, f32[1,8,256,128]{3,2,1,0:T(8,128)S(1)})) conditional(s32[]{:T(128)} %convert_element_type.80, (f32[1,8,256]{2,1,0:T(8,128)S(1)}, f32[1,8,256,128]{3,2,1,0:T(8,128)S(1)}) %tuple.57, (s32[2,512]{1,0:T(2,128)S(1)}, s32[512]{0:T(512)S(1)}, s32[256]{0:T(256)S(1)}, pred[512]{0:T(512)(128)(4,1)S(1)}, ...), branch_computations={%region_4.0_spmd, %region_5.6_spmd} | conditional | flops 544080896 | bytes 11974168 | solution.py:94
  336.2 2.0 fusion.3
  338.2 2.2 fusion.13
  340.5 0.9 and_reduce_fusion.2
  342.1 4.7 %conditional.3 = ((f32[1,8,256]{2,1,0:T(8,128)S(1)}, f32[1,8,256,128]{3,2,1,0:T(8,128)S(1)})) conditional(s32[]{:T(128)} %convert_element_type.80, (f32[1,8,256]{2,1,0:T(8,128)S(1)}, f32[1,8,256,128]{3,2,1,0:T(8,128)S(1)}) %tuple.57, (s32[2,512]{1,0:T(2,128)S(1)}, s32[512]{0:T(512)S(1)}, s32[256]{0:T(256)S(1)}, pred[512]{0:T(512)(128)(4,1)S(1)}, ...), branch_computations={%region_4.0_spmd, %region_5.6_spmd} | conditional | flops 544080896 | bytes 11974168 | solution.py:94
  342.7 2.0 fusion.3
  344.7 2.2 fusion.13
  347.0 0.9 and_reduce_fusion.2
  348.8 0.9 and_reduce_fusion.2
  350.6 0.9 and_reduce_fusion.2
  352.2 0.3 fusion.30
  352.5 0.3 copy.27
  352.9 0.9 copy.34
  (160 shorter events, 7.6 us)
Async XLA Ops:
  6.5 4.7 %copy-start = (s32[2,64]{1,0:T(2,128)S(1)}, s32[2,64]{1,0:T(2,128)}, u32[]{:S(2)}) copy-start(s32[2,64]{1,0:T(2,128)} %param.19) | copy-start | bytes 1540
  6.5 135.6 %all-gather.4.cloned.1.call-start = ((), (), s32[]{:S(2)}) async-start(), calls=%async_computation | async-start | bytes 2162688 | tf_op jit(solution)/shard_map/all_gather | solution.py:52
  10.5 266.3 %all-gather.6.cloned.1.call-start = ((), (), s32[]{:S(2)}) async-start(), calls=%async_computation.1 | async-start | bytes 2162688 | tf_op jit(solution)/shard_map/all_gather | solution.py:53
Sparse Core Ops, SparseCore 0:
  10.6 131.4 all-gather.3
  144.2 132.5 all-gather.5
where the time goes:
time: 361 us
  waiting for transfers between devices  200 us (55%)
  blocking collectives  61.7 us (17%)
  matrix products  41.7 us (12%)
  other arithmetic  25.2 us (7%)
  between operations  13.5 us (4%)
  loops' own time  12.4 us (3%)
  local copies, waits for them, and re-layouts  5.65 us (2%)
    all_gather x1, waiting for transfers between devices, local(): value_part = lax.all_gather(values, 'ctx', axis=0, tiled=True)  135 us
    all_gather x1, waiting for transfers between devices, local(): key_part = lax.all_gather(key_rotated_rows, 'ctx', axis=0, tiled=True)  65.1 us
    all_gather x1, blocking collectives, local(): seg_part = lax.all_gather(seg_send, 'ctx', axis=0, tiled=True)  61.7 us
    dot_general x10, matrix products, compute(): jnp.einsum('kgqj,jkd->kgqd', weight.astype(jnp.bfloat16), value_blk, pref...  21.9 us
    dot_general x10, matrix products, compute(): jnp.einsum('qkgd,jkd->kgqj', query_rotated_rows, key_blk, preferred_eleme...  19.8 us
    reduce_or x16, other arithmetic, one(): return lax.cond(jnp.any(mask), compute, lambda old: old, state)  14.5 us
    another operation x1, loops' own time, local(): total, acc = lax.fori_loop(0, count // sub, one, init)  11.7 us
  transfers between devices with their start and end apart: 2, of which 2 were waited for; matrix products, arithmetic and copies ran while one was open for 1% of the time, Pallas kernels for 0%

commit v1 on v0

v1 whole, which is shorter than its diff:
```python
import functools
import math

import jax
import jax.numpy as jnp
from jax import lax
from jax.experimental import pallas as pl
from jax.experimental.pallas import tpu as pltpu
from jax.sharding import PartitionSpec as P

HEAD = 128
NT = (((1,), (1,)), ((), ()))
VMEM = pl.BlockSpec(memory_space=pltpu.VMEM)
SMEM = pl.BlockSpec(memory_space=pltpu.SMEM)
PARAMS = pltpu.CompilerParams(vmem_limit_bytes=40 * 2**20)
PAD = 16

NEAR, HELD, LOW, HIGH, SKIP, MASKS = 2, 5, 7, 9, 11, 13


def rotate(vec, gain, cosine, sine):
    vec = vec.astype(jnp.float32)
    vec = vec * lax.rsqrt(jnp.mean(vec * vec, axis=-1, keepdims=True) + 1e-06) * gain
    turned = jnp.concatenate([vec[:, HEAD // 2 :], vec[:, : HEAD // 2]], axis=1)
    return vec * cosine + turned * sine


def key_kernel(keys, values, gain, cosine, sine, out):
    rows = keys.shape[0]
    out[:rows, :] = rotate(keys[...], gain[...], cosine[...], sine[...]).astype(out.dtype)
    out[rows:, :] = values[...]


def query_kernel(queries, gain, cosine, sine, mask, out):
    rows = queries.shape[0]
    heads = queries.shape[1] // HEAD
    for head in range(heads):
        part = queries[:, head * HEAD : (head + 1) * HEAD]
        out[head * rows : (head + 1) * rows, :] = rotate(
            part, gain[...], cosine[...], sine[...]
        ).astype(out.dtype)
    out[heads * rows :, :] = jnp.broadcast_to(
        mask[...].astype(jnp.float32), (PAD, HEAD)
    ).astype(out.dtype)


def hold_kernel(info, own, far, below, above, held, *, period):
    plane = info[0] // 2
    size = own.shape[0]

    @pl.when(plane < period)
    def _():
        held[:size, :] = own[...]

    @pl.when(plane >= period)
    def _():
        held[:size, :] = far[...]

    middle = (plane >= period // 2) & (plane < period + period // 2)

    @pl.when(middle)
    def _():
        held[size:, :] = below[...]

    @pl.when(jnp.logical_not(middle))
    def _():
        held[size:, :] = above[...]


def attend_kernel(info, *refs, jobs, near, counts, rows, heads, prompt):
    refs = list(refs)
    starts = refs.pop(0) if near else None
    queries = [refs.pop(0) for _ in jobs]
    states = [refs.pop(0) if job["state"] else None for job in jobs]
    shards = []
    for count in counts:
        ref = refs.pop(0)
        shards += [(ref, part * 2 * rows) for part in range(count)]
    half = rows // 2
    scale = HEAD**-0.5 * math.log2(math.e)
    ones = jnp.ones((rows, HEAD), jnp.bfloat16)

    def partial(query, head, shard, mask):
        ref, at = shard
        score = lax.dot_general(
            query[pl.ds(head * rows, rows), :],
            ref[at : at + rows, :],
            NT,
            preferred_element_type=jnp.float32,
        )
        weight = jnp.exp2(score * scale)
        if mask is not None:
            weight = jnp.where(mask, weight, 0.0)
        extended = jnp.concatenate([ref[at + rows : at + 2 * rows, :], ones], axis=1)
        return jnp.dot(weight.astype(jnp.bfloat16), extended, preferred_element_type=jnp.float32)

    for job, query, state in zip(jobs, queries, states):
        out = refs.pop(0)
        total = refs.pop() if job["pack"] else out
        lane = job["lane"]
        mine = info[lane]

        def block(shard, a, b, lane=lane):
            width = 4 * prompt // rows
            return info[MASKS + lane * 2 * width + a * width + 2 * shard + b]

        some, full = [], []
        for slot in job["slots"]:
            shard = info[slot]
            seen = [block(shard, a, b) > 0 for a in range(2) for b in range(2)]
            any_seen = seen[0] | seen[1] | seen[2] | seen[3]
            if near:
                any_seen = any_seen & (shard * rows >= prompt)
            some.append(any_seen)
            full.append(
                seen[0]
                & seen[1]
                & seen[2]
                & seen[3]
                & (shard < mine)
                & (shard * rows < prompt)
            )
        all_full = functools.reduce(jnp.logical_and, full)

        def together(query=query, state=state, total=total):
            for head in range(heads):
                at = pl.ds(head * rows, rows)
                add = None if state is None else state[at, :]
                for shard in shards:
                    new = partial(query, head, shard, None)
                    add = new if add is None else add + new
                total[at, :] = add

        def one_by_one(
            job=job, query=query, state=state, total=total, mine=mine, some=some, full=full, block=block
        ):
            total[...] = jnp.zeros_like(total) if state is None else state[...]
            for slot, shard, any_seen, all_seen in zip(job["slots"], shards, some, full):

                def add(mask, query=query, shard=shard, total=total):
                    @pl.loop(0, heads // 4)
                    def _(group):
                        for inner in range(4):
                            head = group * 4 + inner
                            at = pl.ds(pl.multiple_of(head * rows, rows), rows)
                            total[at, :] += partial(query, head, shard, mask)

                if not near:

                    @pl.when(all_seen)
                    def _(add=add):
                        add(None)

                @pl.when(any_seen & jnp.logical_not(all_seen))
                def _(slot=slot, add=add):
                    number = info[slot]
                    row = lax.broadcasted_iota(jnp.int32, (rows, rows), 0)
                    column = lax.broadcasted_iota(jnp.int32, (rows, rows), 1)
                    upper = jnp.where(column < half, block(number, 0, 0), block(number, 0, 1))
                    lower = jnp.where(column < half, block(number, 1, 0), block(number, 1, 1))
                    key = number * rows + column
                    mask = (jnp.where(row < half, upper, lower) > 0) & (key <= mine * rows + row)
                    if near:
                        begun = jnp.concatenate([starts[...]] * (rows // HEAD), axis=1)
                        mask = mask & ((key < prompt) | (key >= begun))
                    add(mask)

        if near:
            one_by_one()
        else:
            pl.when(all_full)(together)
            pl.when(jnp.logical_not(all_full))(one_by_one)

        if job["pack"]:
            at_lane = lax.broadcasted_iota(jnp.int32, (rows, HEAD), 1)
            packed = jnp.zeros((rows, HEAD), jnp.float32)
            for head in range(heads):
                at = pl.ds(head * rows, rows)
                out[at, :] = total[at, :HEAD].astype(out.dtype)
                whole = total[at, HEAD:]
                high = whole.astype(jnp.bfloat16).astype(jnp.float32)
                packed = jnp.where(at_lane == head, high, packed)
                packed = jnp.where(at_lane == heads + head, whole - high, packed)
            out[heads * rows :, :] = packed.astype(out.dtype)


def finish_kernel(own, other, out):
    rows = out.shape[0]
    heads = out.shape[1] // HEAD
    packed = other[heads * rows :, :]
    source = lax.broadcasted_iota(jnp.int32, (HEAD, HEAD), 0)
    for head in range(heads):
        at = slice(head * rows, (head + 1) * rows)
        pick = jnp.where((source == head) | (source == heads + head), 1.0, 0.0)
        total = jnp.dot(packed, pick.astype(jnp.bfloat16), preferred_element_type=jnp.float32)
        total = total + own[at, HEAD:]
        value = own[at, :HEAD] + other[at, :].astype(jnp.float32)
        out[:, head * HEAD : (head + 1) * HEAD] = (value / total).astype(out.dtype)


def local(
    queries, keys, values, query_norm_gain, key_norm_gain, positions, segment_ids, block_mask
):
    rows = queries.shape[0]
    heads = queries.shape[1] // HEAD
    ring = lax.axis_size("ctx")
    mine = lax.axis_index("ctx")
    prompt = ring * rows // 2
    depth = ring // 2
    period = depth // 2
    plane, lane = mine // 2, mine % 2
    shape = jax.ShapeDtypeStruct

    def move(array, target):
        pairs = [(z * 2 + y, target(z) % depth * 2 + y) for z in range(depth) for y in range(2) if target(z) is not None]
        return lax.ppermute(array, "ctx", pairs)

    def swap(array):
        return lax.ppermute(array, "ctx", [(c, c ^ 1) for c in range(ring)])

    with jax.named_scope("angles"):
        freq = jnp.exp(
            -math.log(1000000.0) * jnp.arange(HEAD // 2, dtype=jnp.float32) * (2.0 / HEAD)
        )
        freq = jnp.concatenate([freq, freq])
        angle = positions.astype(jnp.float32)[:, None] * freq[None, :]
        sign = jnp.where(jnp.arange(HEAD) < HEAD // 2, -1.0, 1.0).astype(jnp.float32)
        cosine = jnp.cos(angle)
        sine = jnp.sin(angle) * sign[None, :]

    def whole(array_shape):
        return pl.BlockSpec(array_shape, lambda i: (0,) * len(array_shape))

    kv = pl.pallas_call(
        key_kernel,
        grid=(1,),
        out_shape=shape((2 * rows, HEAD), jnp.bfloat16),
        in_specs=[whole((rows, HEAD))] * 2 + [whole((1, HEAD))] + [whole((rows, HEAD))] * 2,
        out_specs=whole((2 * rows, HEAD)),
        compiler_params=PARAMS,
        name="rotate_keys",
    )(keys, values, key_norm_gain[None, :], cosine, sine)

    far = move(kv, lambda z: z + period if z < period else None)
    below = move(kv, lambda z: z + period // 2 if z < period else None)
    above = move(kv, lambda z: z - period // 2 if z < period else None)

    query = pl.pallas_call(
        query_kernel,
        grid=(1,),
        out_shape=shape((heads * rows + PAD, HEAD), jnp.bfloat16),
        in_specs=[whole((rows, heads * HEAD)), whole((1, HEAD))]
        + [whole((rows, HEAD))] * 2
        + [whole((1, HEAD))],
        out_specs=whole((heads * rows + PAD, HEAD)),
        compiler_params=PARAMS,
        name="rotate_queries",
    )(queries, query_norm_gain[None, :], cosine, sine, block_mask.reshape(1, HEAD))
    query_cross = swap(query)

    near1 = lax.ppermute(kv, "ctx", [(c, c + 1) for c in range(ring // 2, ring - 1)])
    near2 = lax.ppermute(kv, "ctx", [(c, c + 2) for c in range(ring // 2, ring - 2)])

    def number(offset):
        return (plane + offset) % period * 2 + lane

    odd = plane % 2
    numbers = [mine, mine + 1 - 2 * lane, mine, mine - 1, mine - 2]
    numbers += [number(o) for o in (0, 4, -1, 3, 1, 5)]
    numbers += [number(2 + 4 * odd), number(6 - 4 * odd)]
    numbers = jnp.stack(numbers).astype(jnp.int32)
    info_own = jnp.concatenate([numbers, block_mask.reshape(-1)])
    index = mine * rows + jnp.arange(rows, dtype=jnp.int32)
    starts = jnp.broadcast_to((index - (positions - prompt))[:, None], (rows, HEAD))

    def attend(info, jobs, queries_in, states, shards, counts, name, near=False):
        out_shape, scratch = [], []
        for job in jobs:
            sums = shape((heads * rows, 2 * HEAD), jnp.float32)
            if job["pack"]:
                scratch.append(pltpu.VMEM(sums.shape, sums.dtype))
                sums = shape((heads * rows + rows, HEAD), jnp.bfloat16)
            out_shape.append(sums)
        inputs = [info] + ([starts] if near else []) + queries_in + states + shards
        work = heads * rows * rows * sum(len(job["slots"]) for job in jobs)
        return pl.pallas_call(
            functools.partial(
                attend_kernel,
                jobs=jobs,
                near=near,
                counts=counts,
                rows=rows,
                heads=heads,
                prompt=prompt,
            ),
            out_shape=out_shape,
            in_specs=[SMEM] + [VMEM] * (len(inputs) - 1),
            out_specs=[VMEM] * len(out_shape),
            scratch_shapes=scratch,
            cost_estimate=pl.CostEstimate(
                flops=8 * HEAD * work, bytes_accessed=4 * heads * rows * HEAD, transcendentals=work
            ),
            compiler_params=PARAMS,
            name=name,
        )(*inputs)

    def job(lane, slots, state, pack=False):
        return dict(lane=lane, slots=slots, state=state, pack=pack)

    (own,) = attend(
        info_own,
        [job(0, [NEAR, NEAR + 1, NEAR + 2], False)],
        [query],
        [],
        [kv, near1, near2],
        [1, 1, 1],
        "attend_near",
        near=True,
    )
    mask_cross = query_cross[heads * rows, :].astype(jnp.int32)
    info = jnp.concatenate([info_own, mask_cross])
    far, below, above, own, query_cross, info = lax.optimization_barrier(
        (far, below, above, own, query_cross, info)
    )

    held = pl.pallas_call(
        functools.partial(hold_kernel, period=period),
        out_shape=shape((4 * rows, HEAD), jnp.bfloat16),
        in_specs=[SMEM] + [VMEM] * 4,
        out_specs=VMEM,
        compiler_params=PARAMS,
        name="hold_shards",
    )(info_own, kv, far, below, above)
    low = move(held, lambda z: z + 1)
    high = move(held, lambda z: z - 1)
    skip = move(held, lambda z: z + 2 if z % 2 else z - 2)

    slots = [HELD, HELD + 1]
    own, cross = attend(
        info,
        [job(0, slots, True), job(1, slots, False)],
        [query, query_cross],
        [own],
        [held],
        [2],
        "attend_held",
    )
    slots = [LOW, LOW + 1, HIGH, HIGH + 1]
    (cross,) = attend(
        info, [job(1, slots, True)], [query_cross], [cross], [low, high], [2, 2], "attend_next_cross"
    )
    last = [SKIP, SKIP + 1]
    (cross,) = attend(
        info, [job(1, last, True, True)], [query_cross], [cross], [skip], [2], "attend_last_cross"
    )
    other = swap(cross)
    (own,) = attend(
        info,
        [job(0, slots + last, True)],
        [query],
        [own],
        [low, high, skip],
        [2, 2, 2],
        "attend_last",
    )
    return pl.pallas_call(
        finish_kernel,
        out_shape=shape((rows, heads * HEAD), jnp.bfloat16),
        in_specs=[VMEM] * 2,
        out_specs=VMEM,
        compiler_params=PARAMS,
        name="finish",
    )(own, other)


def solution(mesh):
    return jax.shard_map(
        local,
        mesh=mesh,
        in_specs=(
            P(("dp", "ctx"), "tp"),
            P(("dp", "ctx"), "tp"),
            P(("dp", "ctx"), "tp"),
            P(),
            P(),
            P(("dp", "ctx")),
            P(("dp", "ctx")),
            P(("dp", "ctx"), None),
        ),
        out_specs=P(("dp", "ctx"), "tp"),
        check_vma=False,
    )
```

time: 361 us -> 92 us (0.25)
  the two profiles are of different devices: /device:TPU:384 before, /device:TPU:2 now
where the time goes in v1:
time: 92 us; the launch traced here: 91.5 us
  starting transfers between devices  44.3 us (48%)
  waiting for transfers between devices  27.5 us (30%)
  Pallas kernels  9.85 us (11%)
  local copies, waits for them, and re-layouts  8.04 us (9%)
  other arithmetic  1.38 us (2%)
    ppermute x6, starting transfers between devices, move(): return lax.ppermute(array, 'ctx', pairs)  36.9 us
    ppermute x6, waiting for transfers between devices, move(): return lax.ppermute(array, 'ctx', pairs)  15.8 us
    ppermute x2, waiting for transfers between devices, swap(): return lax.ppermute(array, 'ctx', [(c, c ^ 1) for c in range(ring)])  11.7 us
    unnamed x16, local copies, waits for them, and re-layouts  6.93 us
    pallas_call x5, Pallas kernels, attend(): pl.pallas_call(functools.partial(attend_kernel, jobs=jobs, near=near, cou...  6.79 us
    ppermute x2, starting transfers between devices, swap(): return lax.ppermute(array, 'ctx', [(c, c ^ 1) for c in range(ring)])  6.05 us
  transfers between devices with their start and end apart: 10, of which 3 were waited for; matrix products, arithmetic and copies ran while one was open for 0% of the time, Pallas kernels for 7%

profile of v1, /device:TPU:2, one launch (start us, length us, event | category | flops | bytes accessed | tf_op | source)
XLA Modules:
  0.0 91.5 jit_solution(16924955106150464957)
XLA Ops:
  0.0 0.0 copy-start.7
  0.0 0.1 compare_select_fusion
  0.1 0.8 reshape.17.mask
  0.9 0.8 add_subtract_fusion
  1.6 0.5 fusion
  2.2 0.0 copy-start
  2.2 1.0 %copy-done = bf16[256,1024]{1,0:T(8,128)(2,1)S(1)} copy-done((bf16[256,1024]{1,0:T(8,128)(2,1)S(1)}, bf16[256,1024]{1,0:T(8,128)(2,1)}, u32[]{:S(2)}) %copy-start) | copy-done | bytes 524312
  3.2 0.0 copy-start.3
  3.2 0.7 copy-done.3
  3.9 1.1 %rotate_queries.1.refs_1_.refs_0_ = bf16[2064,128]{1,0:T(8,128)(2,1)S(1)} custom-call(bf16[256,1024]{1,0:T(8,128)(2,1)S(1)} %copy-done, f32[1,128]{1,0:T(1,128)S(1)} %bitcast.19, f32[256,128]{1,0:T(8,128)S(1)} %get-tuple-element.22.cosine, f32[256,128]{1,0:T(8,128)S(1)} %get-tuple-element.21.sine, s32[1,128]{1,0:T(1,128)S(1)} %reshape.17.mask), custom_call_target="tpu_custom_call" | custom-call | tf_op jit(solution)/shard_map/rotate_queries/pallas_call | solution.py:248
  5.0 3.5 %collective-permute-start.5 = (bf16[2064,128]{1,0:T(8,128)(2,1)S(1)}, bf16[2064,128]{1,0:T(8,128)(2,1)S(1)}, u32[]{:S(2)}, u32[]{:S(2)}) collective-permute-start(bf16[2064,128]{1,0:T(8,128)(2,1)S(1)} %rotate_queries.1.refs_1_.refs_0_), channel_id=1, source_target_pairs={{0,8},{8,0},{16,24},{24,16},{32,40},{40,32},{48,56},{56,48},{64,72... | collective-permute-start | bytes 1585160 | tf_op jit(solution)/shard_map/ppermute | solution.py:219
  8.5 0.0 copy-start.1
  8.5 0.8 copy-done.1
  9.3 0.0 copy-start.2
  9.3 0.8 copy-done.2
  10.2 0.0 copy-start.4
  10.2 0.7 copy-done.4
  10.8 0.2 rotate_keys.1.refs_2_.own
  11.0 0.7 collective-permute-start.3
  11.7 0.7 collective-permute-start.4
  12.4 19.7 %collective-permute-start = (bf16[512,128]{1,0:T(8,128)(2,1)S(1)}, bf16[512,128]{1,0:T(8,128)(2,1)S(1)}, u32[]{:S(2)}, u32[]{:S(2)}) collective-permute-start(bf16[512,128]{1,0:T(8,128)(2,1)S(1)} %rotate_keys.1.refs_2_.own), channel_id=1, source_target_pairs={{0,128},{8,136},{16,144},{24,152},{32,160},{40,168},{48,176},{56,1... | collective-permute-start | bytes 393224 | tf_op jit(solution)/shard_map/ppermute | solution.py:216
  32.1 4.3 %collective-permute-start.1 = (bf16[512,128]{1,0:T(8,128)(2,1)S(1)}, bf16[512,128]{1,0:T(8,128)(2,1)S(1)}, u32[]{:S(2)}, u32[]{:S(2)}) collective-permute-start(bf16[512,128]{1,0:T(8,128)(2,1)S(1)} %rotate_keys.1.refs_2_.own), channel_id=1, source_target_pairs={{0,64},{8,72},{16,80},{24,88},{32,96},{40,104},{48,112},{56,120},{... | collective-permute-start | bytes 393224 | tf_op jit(solution)/shard_map/ppermute | solution.py:216
  36.5 0.0 copy-done.7
  36.5 0.1 reshape.16
  36.6 0.1 concatenate.11.info
  36.7 0.0 collective-permute-done.3.refs_3_
  36.7 1.9 %collective-permute-start.2 = (bf16[512,128]{1,0:T(8,128)(2,1)S(1)}, bf16[512,128]{1,0:T(8,128)(2,1)S(1)}, u32[]{:S(2)}, u32[]{:S(2)}) collective-permute-start(bf16[512,128]{1,0:T(8,128)(2,1)S(1)} %rotate_keys.1.refs_2_.own), channel_id=1, source_target_pairs={{0,192},{8,200},{16,208},{24,216},{32,224},{40,232},{48,240},{56,2... | collective-permute-start | bytes 393224 | tf_op jit(solution)/shard_map/ppermute | solution.py:216
  38.7 0.0 collective-permute-done.4.refs_4_
  38.7 0.1 broadcast_in_dim.26.refs_0_
  38.8 0.7 attend_near.1.refs_2_
  39.5 0.0 copy-start.5
  39.5 1.3 %copy-done.5 = f32[2048,256]{1,0:T(8,128)} copy-done((f32[2048,256]{1,0:T(8,128)}, f32[2048,256]{1,0:T(8,128)S(1)}, u32[]{:S(2)}) %copy-start.5) | copy-done | bytes 2097176
  40.8 0.0 collective-permute-done.5.refs_1_.refs_0_
  40.8 0.1 concatenate.12.info
  40.9 0.0 collective-permute-done.far
  40.9 0.0 collective-permute-done.1.below
  40.9 14.0 %collective-permute-done.2.above = bf16[512,128]{1,0:T(8,128)(2,1)S(1)} collective-permute-done((bf16[512,128]{1,0:T(8,128)(2,1)S(1)}, bf16[512,128]{1,0:T(8,128)(2,1)S(1)}, u32[]{:S(2)}, u32[]{:S(2)}) %collective-permute-start.2) | collective-permute-done | bytes 131104 | tf_op jit(solution)/shard_map/ppermute | solution.py:216
  54.9 0.6 hold_shards.1.refs_3_
  55.5 1.9 %collective-permute-start.6 = (bf16[1024,128]{1,0:T(8,128)(2,1)S(1)}, bf16[1024,128]{1,0:T(8,128)(2,1)S(1)}, u32[]{:S(2)}, u32[]{:S(2)}) collective-permute-start(bf16[1024,128]{1,0:T(8,128)(2,1)S(1)} %hold_shards.1.refs_3_), channel_id=1, source_target_pairs={{0,16},{8,24},{16,32},{24,40},{32,48},{40,56},{48,64},{56,72},{64,... | collective-permute-start | bytes 786440 | tf_op jit(solution)/shard_map/ppermute | solution.py:216
  57.4 5.1 %collective-permute-start.7 = (bf16[1024,128]{1,0:T(8,128)(2,1)S(1)}, bf16[1024,128]{1,0:T(8,128)(2,1)S(1)}, u32[]{:S(2)}, u32[]{:S(2)}) collective-permute-start(bf16[1024,128]{1,0:T(8,128)(2,1)S(1)} %hold_shards.1.refs_3_), channel_id=1, source_target_pairs={{0,240},{8,248},{16,0},{24,8},{32,16},{40,24},{48,32},{56,40},{64,... | collective-permute-start | bytes 786440 | tf_op jit(solution)/shard_map/ppermute | solution.py:216
  62.6 4.0 %collective-permute-start.8 = (bf16[1024,128]{1,0:T(8,128)(2,1)S(1)}, bf16[1024,128]{1,0:T(8,128)(2,1)S(1)}, u32[]{:S(2)}, u32[]{:S(2)}) collective-permute-start(bf16[1024,128]{1,0:T(8,128)(2,1)S(1)} %hold_shards.1.refs_3_), channel_id=1, source_target_pairs={{0,224},{8,232},{16,48},{24,56},{32,0},{40,8},{48,80},{56,88},{64,... | collective-permute-start | bytes 786440 | tf_op jit(solution)/shard_map/ppermute | solution.py:216
  66.5 0.0 copy-start.6
  66.5 1.6 %copy-done.6 = f32[2048,256]{1,0:T(8,128)S(1)} copy-done((f32[2048,256]{1,0:T(8,128)S(1)}, f32[2048,256]{1,0:T(8,128)}, u32[]{:S(2)}) %copy-start.6) | copy-done | bytes 2097176
  68.1 3.1 %attend_held.1 = (f32[2048,256]{1,0:T(8,128)S(1)}, f32[2048,256]{1,0:T(8,128)S(1)}) custom-call(s32[269]{0:T(512)S(1)} %concatenate.12.info, bf16[2064,128]{1,0:T(8,128)(2,1)S(1)} %rotate_queries.1.refs_1_.refs_0_, bf16[2064,128]{1,0:T(8,128)(2,1)S(1)} %collective-permute-done.5.refs_1_.refs_0_, f32[2048,256]{1,0:T(8,128)S(1)} %copy-done.6, ...), custom_call_target="tpu_custom_call" | custom-call | flops 2147483648 | bytes 1048576 | tf_op jit(solution)/shard_map/attend_held/pallas_call | solution.py:286
  71.3 0.0 collective-permute-done.6.refs_2_
  71.3 1.8 %collective-permute-done.7.refs_3_ = bf16[1024,128]{1,0:T(8,128)(2,1)S(1)} collective-permute-done((bf16[1024,128]{1,0:T(8,128)(2,1)S(1)}, bf16[1024,128]{1,0:T(8,128)(2,1)S(1)}, u32[]{:S(2)}, u32[]{:S(2)}) %collective-permute-start.7) | collective-permute-done | bytes 262176 | tf_op jit(solution)/shard_map/ppermute | solution.py:216
  73.0 1.0 %attend_next_cross.1.refs_1_ = f32[2048,256]{1,0:T(8,128)S(1)} custom-call(s32[269]{0:T(512)S(1)} %concatenate.12.info, bf16[2064,128]{1,0:T(8,128)(2,1)S(1)} %collective-permute-done.5.refs_1_.refs_0_, f32[2048,256]{1,0:T(8,128)S(1)} %get-tuple-element.20.refs_1_, bf16[1024,128]{1,0:T(8,128)(2,1)S(1)} %collective-permute-done.6.refs_2_, ...), custom_call_target="tpu_custom_call" | custom-call | flops 2147483648 | bytes 1048576 | tf_op jit(solution)/shard_map/attend_next_cross/pallas_call | solution.py:286
  74.0 0.0 collective-permute-done.8.refs_4_.refs_2_
  74.0 1.0 %attend_last_cross.1 = bf16[2304,128]{1,0:T(8,128)(2,1)S(1)} custom-call(s32[269]{0:T(512)S(1)} %concatenate.12.info, bf16[2064,128]{1,0:T(8,128)(2,1)S(1)} %collective-permute-done.5.refs_1_.refs_0_, f32[2048,256]{1,0:T(8,128)S(1)} %attend_next_cross.1.refs_1_, bf16[1024,128]{1,0:T(8,128)(2,1)S(1)} %collective-permute-done.8.refs_4_.refs_2_), custom_call_target="tpu_custom_call" | custom-call | flops 1073741824 | bytes 1048576 | tf_op jit(solution)/shard_map/attend_last_cross/pallas_call | solution.py:286
  75.0 2.6 %collective-permute-start.9 = (bf16[2304,128]{1,0:T(8,128)(2,1)S(1)}, bf16[2304,128]{1,0:T(8,128)(2,1)S(1)}, u32[]{:S(2)}, u32[]{:S(2)}) collective-permute-start(bf16[2304,128]{1,0:T(8,128)(2,1)S(1)} %attend_last_cross.1), channel_id=1, source_target_pairs={{0,8},{8,0},{16,24},{24,16},{32,40},{40,32},{48,56},{56,48},{64,72... | collective-permute-start | bytes 1769480 | tf_op jit(solution)/shard_map/ppermute | solution.py:219
  77.6 1.0 %attend_last.1.own = f32[2048,256]{1,0:T(8,128)S(1)} custom-call(s32[269]{0:T(512)S(1)} %concatenate.12.info, bf16[2064,128]{1,0:T(8,128)(2,1)S(1)} %rotate_queries.1.refs_1_.refs_0_, f32[2048,256]{1,0:T(8,128)S(1)} %get-tuple-element.19.refs_1_, bf16[1024,128]{1,0:T(8,128)(2,1)S(1)} %collective-permute-done.6.refs_2_, ...), custom_call_target="tpu_custom_call" | custom-call | flops 3221225472 | bytes 1048576 | tf_op jit(solution)/shard_map/attend_last/pallas_call | solution.py:286
  78.6 11.7 %collective-permute-done.9.other = bf16[2304,128]{1,0:T(8,128)(2,1)S(1)} collective-permute-done((bf16[2304,128]{1,0:T(8,128)(2,1)S(1)}, bf16[2304,128]{1,0:T(8,128)(2,1)S(1)}, u32[]{:S(2)}, u32[]{:S(2)}) %collective-permute-start.9) | collective-permute-done | bytes 589856 | tf_op jit(solution)/shard_map/ppermute | solution.py:219
  90.3 1.1 %finish.1 = bf16[256,1024]{1,0:T(8,128)(2,1)} custom-call(f32[2048,256]{1,0:T(8,128)S(1)} %attend_last.1.own, bf16[2304,128]{1,0:T(8,128)(2,1)S(1)} %collective-permute-done.9.other), custom_call_target="tpu_custom_call" | custom-call | tf_op jit(solution)/shard_map/finish/pallas_call | solution.py:366
  (2 shorter events, 0.0 us)
Async XLA Ops:
  0.0 36.5 %copy-start.7 = (s32[2,64]{1,0:T(2,128)S(1)}, s32[2,64]{1,0:T(2,128)}, u32[]{:S(2)}) copy-start(s32[2,64]{1,0:T(2,128)} %param.14) | copy-start | bytes 1540
  2.2 1.0 %copy-start = (bf16[256,1024]{1,0:T(8,128)(2,1)S(1)}, bf16[256,1024]{1,0:T(8,128)(2,1)}, u32[]{:S(2)}) copy-start(bf16[256,1024]{1,0:T(8,128)(2,1)} %queries.1) | copy-start | bytes 1572868
  3.2 0.7 copy-start.3
  5.0 35.8 %collective-permute-start.5 = (bf16[2064,128]{1,0:T(8,128)(2,1)S(1)}, bf16[2064,128]{1,0:T(8,128)(2,1)S(1)}, u32[]{:S(2)}, u32[]{:S(2)}) collective-permute-start(bf16[2064,128]{1,0:T(8,128)(2,1)S(1)} %rotate_queries.1.refs_1_.refs_0_), channel_id=1, source_target_pairs={{0,8},{8,0},{16,24},{24,16},{32,40},{40,32},{48,56},{56,48},{64,72... | collective-permute-start | bytes 1585160 | tf_op jit(solution)/shard_map/ppermute | solution.py:219
  8.5 0.8 copy-start.1
  9.3 0.8 copy-start.2
  10.2 0.7 copy-start.4
  11.0 25.7 %collective-permute-start.3 = (bf16[512,128]{1,0:T(8,128)(2,1)S(1)}, bf16[512,128]{1,0:T(8,128)(2,1)S(1)}, u32[]{:S(2)}, u32[]{:S(2)}) collective-permute-start(bf16[512,128]{1,0:T(8,128)(2,1)S(1)} %rotate_keys.1.refs_2_.own), channel_id=1, source_target_pairs={{128,136},{136,144},{144,152},{152,160},{160,168},{168,176},{176,1... | collective-permute-start | bytes 393224 | tf_op jit(solution)/shard_map/ppermute | solution.py:261
  11.7 27.0 %collective-permute-start.4 = (bf16[512,128]{1,0:T(8,128)(2,1)S(1)}, bf16[512,128]{1,0:T(8,128)(2,1)S(1)}, u32[]{:S(2)}, u32[]{:S(2)}) collective-permute-start(bf16[512,128]{1,0:T(8,128)(2,1)S(1)} %rotate_keys.1.refs_2_.own), channel_id=1, source_target_pairs={{128,144},{136,152},{144,160},{152,168},{160,176},{168,184},{176,1... | collective-permute-start | bytes 393224 | tf_op jit(solution)/shard_map/ppermute | solution.py:262
  12.4 28.5 %collective-permute-start = (bf16[512,128]{1,0:T(8,128)(2,1)S(1)}, bf16[512,128]{1,0:T(8,128)(2,1)S(1)}, u32[]{:S(2)}, u32[]{:S(2)}) collective-permute-start(bf16[512,128]{1,0:T(8,128)(2,1)S(1)} %rotate_keys.1.refs_2_.own), channel_id=1, source_target_pairs={{0,128},{8,136},{16,144},{24,152},{32,160},{40,168},{48,176},{56,1... | collective-permute-start | bytes 393224 | tf_op jit(solution)/shard_map/ppermute | solution.py:216
  32.1 8.9 %collective-permute-start.1 = (bf16[512,128]{1,0:T(8,128)(2,1)S(1)}, bf16[512,128]{1,0:T(8,128)(2,1)S(1)}, u32[]{:S(2)}, u32[]{:S(2)}) collective-permute-start(bf16[512,128]{1,0:T(8,128)(2,1)S(1)} %rotate_keys.1.refs_2_.own), channel_id=1, source_target_pairs={{0,64},{8,72},{16,80},{24,88},{32,96},{40,104},{48,112},{56,120},{... | collective-permute-start | bytes 393224 | tf_op jit(solution)/shard_map/ppermute | solution.py:216
  36.7 18.2 %collective-permute-start.2 = (bf16[512,128]{1,0:T(8,128)(2,1)S(1)}, bf16[512,128]{1,0:T(8,128)(2,1)S(1)}, u32[]{:S(2)}, u32[]{:S(2)}) collective-permute-start(bf16[512,128]{1,0:T(8,128)(2,1)S(1)} %rotate_keys.1.refs_2_.own), channel_id=1, source_target_pairs={{0,192},{8,200},{16,208},{24,216},{32,224},{40,232},{48,240},{56,2... | collective-permute-start | bytes 393224 | tf_op jit(solution)/shard_map/ppermute | solution.py:216
  39.5 1.3 %copy-start.5 = (f32[2048,256]{1,0:T(8,128)}, f32[2048,256]{1,0:T(8,128)S(1)}, u32[]{:S(2)}) copy-start(f32[2048,256]{1,0:T(8,128)S(1)} %attend_near.1.refs_2_) | copy-start | bytes 6291460
  55.5 15.8 %collective-permute-start.6 = (bf16[1024,128]{1,0:T(8,128)(2,1)S(1)}, bf16[1024,128]{1,0:T(8,128)(2,1)S(1)}, u32[]{:S(2)}, u32[]{:S(2)}) collective-permute-start(bf16[1024,128]{1,0:T(8,128)(2,1)S(1)} %hold_shards.1.refs_3_), channel_id=1, source_target_pairs={{0,16},{8,24},{16,32},{24,40},{32,48},{40,56},{48,64},{56,72},{64,... | collective-permute-start | bytes 786440 | tf_op jit(solution)/shard_map/ppermute | solution.py:216
  57.4 15.6 %collective-permute-start.7 = (bf16[1024,128]{1,0:T(8,128)(2,1)S(1)}, bf16[1024,128]{1,0:T(8,128)(2,1)S(1)}, u32[]{:S(2)}, u32[]{:S(2)}) collective-permute-start(bf16[1024,128]{1,0:T(8,128)(2,1)S(1)} %hold_shards.1.refs_3_), channel_id=1, source_target_pairs={{0,240},{8,248},{16,0},{24,8},{32,16},{40,24},{48,32},{56,40},{64,... | collective-permute-start | bytes 786440 | tf_op jit(solution)/shard_map/ppermute | solution.py:216
  62.6 11.5 %collective-permute-start.8 = (bf16[1024,128]{1,0:T(8,128)(2,1)S(1)}, bf16[1024,128]{1,0:T(8,128)(2,1)S(1)}, u32[]{:S(2)}, u32[]{:S(2)}) collective-permute-start(bf16[1024,128]{1,0:T(8,128)(2,1)S(1)} %hold_shards.1.refs_3_), channel_id=1, source_target_pairs={{0,224},{8,232},{16,48},{24,56},{32,0},{40,8},{48,80},{56,88},{64,... | collective-permute-start | bytes 786440 | tf_op jit(solution)/shard_map/ppermute | solution.py:216
  66.5 1.6 %copy-start.6 = (f32[2048,256]{1,0:T(8,128)S(1)}, f32[2048,256]{1,0:T(8,128)}, u32[]{:S(2)}) copy-start(f32[2048,256]{1,0:T(8,128)} %copy-done.5) | copy-start | bytes 6291460
  75.0 15.3 %collective-permute-start.9 = (bf16[2304,128]{1,0:T(8,128)(2,1)S(1)}, bf16[2304,128]{1,0:T(8,128)(2,1)S(1)}, u32[]{:S(2)}, u32[]{:S(2)}) collective-permute-start(bf16[2304,128]{1,0:T(8,128)(2,1)S(1)} %attend_last_cross.1), channel_id=1, source_target_pairs={{0,8},{8,0},{16,24},{24,16},{32,40},{40,32},{48,56},{56,48},{64,72... | collective-permute-start | bytes 1769480 | tf_op jit(solution)/shard_map/ppermute | solution.py:219

commit v2 on v1

v2 whole, which is shorter than its diff:
```python
import functools
import math

import jax
import jax.numpy as jnp
import numpy as np
from jax import lax
from jax.experimental import pallas as pl
from jax.experimental.pallas import tpu as pltpu
from jax.sharding import PartitionSpec as P

HEAD = 128
NT = (((1,), (1,)), ((), ()))
HBM = pl.BlockSpec(memory_space=pltpu.HBM)
VMEM = pl.BlockSpec(memory_space=pltpu.VMEM)
SMEM = pl.BlockSpec(memory_space=pltpu.SMEM)
PARAMS = pltpu.CompilerParams(vmem_limit_bytes=40 * 2**20)
COST = pl.CostEstimate(flops=1, bytes_accessed=1, transcendentals=0)
CHOOSE = 10**10
PAD = 16
PART = 128

NEAR, HELD, LOW, HIGH, SKIP, MASKS = 2, 4, 6, 8, 10, 12


def rotate(vec, gain, cosine, sine):
    vec = vec.astype(jnp.float32)
    vec = vec * lax.rsqrt(jnp.mean(vec * vec, axis=-1, keepdims=True) + 1e-06) * gain
    turned = jnp.concatenate([vec[:, HEAD // 2 :], vec[:, : HEAD // 2]], axis=1)
    return vec * cosine + turned * sine


def cos_sin(angle):
    turns = jnp.floor(angle * (2 / math.pi) + 0.5)
    rest = angle - turns * 1.5703125
    rest = rest - turns * 4.837512969970703e-4
    rest = rest - turns * 7.549789954891882e-8
    square = rest * rest
    sine = -1.9515295891e-4 * square + 8.3321608736e-3
    sine = (sine * square - 1.6666654611e-1) * square * rest + rest
    cosine = 2.443315711809948e-5 * square - 1.388731625493765e-3
    cosine = (cosine * square + 4.166664568298827e-2) * square * square - 0.5 * square + 1.0
    quarter = turns.astype(jnp.int32)
    odd = (quarter & 1) == 1
    swapped_sine = jnp.where(odd, cosine, sine)
    swapped_cosine = jnp.where(odd, sine, cosine)
    sine = jnp.where((quarter & 2) == 2, -swapped_sine, swapped_sine)
    cosine = jnp.where(((quarter + 1) & 2) == 2, -swapped_cosine, swapped_cosine)
    return cosine, sine


def key_kernel(keys, values, gain, positions, freq, out, cosine, sine, key_at, gain_at, pos_at, freq_at, sems):
    rows = keys.shape[0]
    copies = [
        pltpu.make_async_copy(source, target, sems.at[i])
        for i, (source, target) in enumerate(
            [
                (positions, pos_at),
                (freq, freq_at),
                (keys, key_at),
                (gain, gain_at),
                (values, out.at[pl.ds(rows, rows), :]),
            ]
        )
    ]
    for copy in copies:
        copy.start()
    copies[0].wait()
    copies[1].wait()
    place = jnp.broadcast_to(pos_at[...].astype(jnp.float32), (HEAD, rows)).T
    cos, sin = cos_sin(place * freq_at[...])
    lane = lax.broadcasted_iota(jnp.int32, (rows, HEAD), 1)
    sin = jnp.where(lane < HEAD // 2, -sin, sin)
    cosine[...] = cos
    sine[...] = sin
    copies[2].wait()
    copies[3].wait()
    out[:rows, :] = rotate(key_at[...], gain_at[...], cos, sin).astype(out.dtype)
    copies[4].wait()


def query_kernel(
    queries, gain, cosine, sine, mask, positions, out, query_at, gain_at, cos_at, sin_at, mask_at, pos_at, sems
):
    rows = queries.shape[0]
    heads = queries.shape[1] // HEAD
    sources = [mask, positions, gain, cosine, sine, queries]
    targets = [mask_at, pos_at, gain_at, cos_at, sin_at, query_at]
    copies = [
        pltpu.make_async_copy(source, target, sems.at[i])
        for i, (source, target) in enumerate(zip(sources, targets))
    ]
    for copy in copies:
        copy.start()
    copies[0].wait()
    copies[1].wait()
    line = mask_at[...].astype(jnp.float32)
    place = pos_at[...]
    high = (place >> 7).astype(jnp.float32)
    low = (place & (PART - 1)).astype(jnp.float32)
    lines = [jnp.concatenate([line[:1, :], line[1:, :]], axis=1)]
    lines += [part[:, at : at + HEAD] for part in (high, low) for at in range(0, rows, HEAD)]
    lines += [jnp.zeros((PAD - len(lines), HEAD), jnp.float32)]
    out[heads * rows :, :] = jnp.concatenate(lines, axis=0).astype(out.dtype)
    for copy in copies[2:]:
        copy.wait()
    for head in range(heads):
        part = query_at[:, head * HEAD : (head + 1) * HEAD]
        out[head * rows : (head + 1) * rows, :] = rotate(
            part, gain_at[...], cos_at[...], sin_at[...]
        ).astype(out.dtype)


def choose_kernel(info, inside, across, out, *, period):
    @pl.when(info[0] // 2 < period)
    def _():
        out[...] = inside[...]

    @pl.when(info[0] // 2 >= period)
    def _():
        out[...] = across[...]


def hold_kernel(info, own, opposite, second, held, *, period):
    size = own.shape[0]

    @pl.when(info[0] // 2 < period)
    def _():
        held[:size, :] = own[...]

    @pl.when(info[0] // 2 >= period)
    def _():
        held[:size, :] = second[...]

    held[size:, :] = opposite[...]


def attend_kernel(info, *refs, jobs, slots, counts, rows, heads, prompt):
    refs = list(refs)
    queries = [refs.pop(0) for _ in jobs]
    states = [refs.pop(0) if job["state"] else None for job in jobs]
    shards = []
    for count in counts:
        ref = refs.pop(0)
        shards += [(ref, part * 2 * rows) for part in range(count)]
    half = rows // 2
    scale = HEAD**-0.5 * math.log2(math.e)
    ones = jnp.ones((rows, HEAD), jnp.bfloat16)

    def partial(query, head, shard, mask):
        ref, at = shard
        score = lax.dot_general(
            query[pl.ds(head * rows, rows), :],
            ref[at : at + rows, :],
            NT,
            preferred_element_type=jnp.float32,
        )
        weight = jnp.exp2(score * scale)
        if mask is not None:
            weight = jnp.where(mask, weight, 0.0)
        extended = jnp.concatenate([ref[at + rows : at + 2 * rows, :], ones], axis=1)
        return jnp.dot(weight.astype(jnp.bfloat16), extended, preferred_element_type=jnp.float32)

    for job, query, state in zip(jobs, queries, states):
        out = refs.pop(0)
        total = refs.pop() if job["pack"] else out
        lane = job["lane"]
        mine = info[lane]

        def block(shard, a, b, lane=lane):
            width = 4 * prompt // rows
            return info[MASKS + lane * 2 * width + a * width + 2 * shard + b]

        early, late = [], []
        for (slot, near), shard in zip(slots, shards):
            number = info[slot]
            seen = [block(number, a, b) > 0 for a in range(2) for b in range(2)]
            any_seen = seen[0] | seen[1] | seen[2] | seen[3]
            if near:
                late.append((shard, number, any_seen & (number * rows >= prompt)))
            else:
                all_seen = seen[0] & seen[1] & seen[2] & seen[3]
                all_seen = all_seen & (number < mine) & (number * rows < prompt)
                early.append((shard, number, any_seen, all_seen))

        def add(shard, mask, query=query, total=total):
            @pl.loop(0, heads // 4)
            def _(group):
                for inner in range(4):
                    head = group * 4 + inner
                    at = pl.ds(pl.multiple_of(head * rows, rows), rows)
                    total[at, :] += partial(query, head, shard, mask)

        def add_masked(shard, number, near, add=add, block=block, query=query, mine=mine):
            row = lax.broadcasted_iota(jnp.int32, (rows, rows), 0)
            column = lax.broadcasted_iota(jnp.int32, (rows, rows), 1)
            upper = jnp.where(column < half, block(number, 0, 0), block(number, 0, 1))
            lower = jnp.where(column < half, block(number, 1, 0), block(number, 1, 1))
            key = number * rows + column
            mask = (jnp.where(row < half, upper, lower) > 0) & (key <= mine * rows + row)
            if near:
                lines = query[heads * rows :, :].astype(jnp.float32)
                count = rows // HEAD
                place = jnp.concatenate(
                    [lines[1 + i : 2 + i, :] * PART + lines[1 + count + i : 2 + count + i, :] for i in range(count)],
                    axis=1,
                )
                offset = jnp.broadcast_to(place - prompt, (rows, rows)).T.astype(jnp.int32)
                mask = mask & ((key < prompt) | (key >= mine * rows + row - offset))
            add(shard, mask)

        def together(query=query, state=state, total=total, early=early):
            for head in range(heads):
                at = pl.ds(head * rows, rows)
                sums = None if state is None else state[at, :]
                for shard, *_ in early:
                    new = partial(query, head, shard, None)
                    sums = new if sums is None else sums + new
                total[at, :] = sums

        def one_by_one(state=state, total=total, early=early, add=add, add_masked=add_masked):
            total[...] = jnp.zeros_like(total) if state is None else state[...]
            for shard, number, any_seen, all_seen in early:
                pl.when(all_seen)(functools.partial(add, shard, None))
                pl.when(any_seen & jnp.logical_not(all_seen))(
                    functools.partial(add_masked, shard, number, False)
                )

        if early:
            all_full = functools.reduce(jnp.logical_and, [entry[3] for entry in early])
            pl.when(all_full)(together)
            pl.when(jnp.logical_not(all_full))(one_by_one)
        else:
            one_by_one()
        for shard, number, any_seen in late:
            pl.when(any_seen)(functools.partial(add_masked, shard, number, True))

        if job["pack"]:
            at_lane = lax.broadcasted_iota(jnp.int32, (rows, HEAD), 1)
            packed = jnp.zeros((rows, HEAD), jnp.float32)
            for head in range(heads):
                at = pl.ds(head * rows, rows)
                out[at, :] = total[at, :HEAD].astype(out.dtype)
                whole = total[at, HEAD:]
                high = whole.astype(jnp.bfloat16).astype(jnp.float32)
                packed = jnp.where(at_lane == head, high, packed)
                packed = jnp.where(at_lane == heads + head, whole - high, packed)
            turned = packed.T[: 2 * heads, :].astype(out.dtype)
            for part in range(rows // HEAD):
                at = pl.ds(heads * rows + part * 2 * heads, 2 * heads)
                out[at, :] = turned[:, part * HEAD : (part + 1) * HEAD]


def finish_kernel(own, other, out):
    rows = out.shape[0]
    heads = out.shape[1] // HEAD
    base = heads * rows
    packed = jnp.concatenate(
        [other[base + p * 2 * heads : base + (p + 1) * 2 * heads, :] for p in range(rows // HEAD)],
        axis=1,
    )
    source = lax.broadcasted_iota(jnp.int32, (2 * heads, HEAD), 0)
    for head in range(heads):
        at = slice(head * rows, (head + 1) * rows)
        pick = jnp.where((source == head) | (source == heads + head), 1.0, 0.0)
        total = lax.dot_general(
            packed,
            pick.astype(jnp.bfloat16),
            (((0,), (0,)), ((), ())),
            preferred_element_type=jnp.float32,
        )
        total = total + own[at, HEAD:]
        value = own[at, :HEAD] + other[at, :].astype(jnp.float32)
        out[:, head * HEAD : (head + 1) * HEAD] = (value / total).astype(out.dtype)


def local(
    queries, keys, values, query_norm_gain, key_norm_gain, positions, segment_ids, block_mask
):
    rows = queries.shape[0]
    heads = queries.shape[1] // HEAD
    ring = lax.axis_size("ctx")
    mine = lax.axis_index("ctx")
    prompt = ring * rows // 2
    depth = ring // 2
    period = depth // 2
    plane, lane = mine // 2, mine % 2
    shape = jax.ShapeDtypeStruct

    def move(array, target):
        pairs = [(z * 2 + y, target(z) % depth * 2 + y) for z in range(depth) for y in range(2) if target(z) is not None]
        return lax.ppermute(array, "ctx", pairs)

    def swap(array):
        return lax.ppermute(array, "ctx", [(c, c ^ 1) for c in range(ring)])

    freq = 1000000.0 ** (-2.0 * (np.arange(HEAD) % (HEAD // 2)) / HEAD)
    freq = jnp.asarray(freq[None, :], jnp.float32)
    kv, cosine, sine = pl.pallas_call(
        key_kernel,
        out_shape=[
            shape((2 * rows, HEAD), jnp.bfloat16),
            shape((rows, HEAD), jnp.float32),
            shape((rows, HEAD), jnp.float32),
        ],
        in_specs=[HBM] * 5,
        out_specs=[VMEM] * 3,
        scratch_shapes=[
            pltpu.VMEM((rows, HEAD), jnp.bfloat16),
            pltpu.VMEM((1, HEAD), jnp.float32),
            pltpu.VMEM((1, rows), jnp.int32),
            pltpu.VMEM((1, HEAD), jnp.float32),
            pltpu.SemaphoreType.DMA((5,)),
        ],
        cost_estimate=COST,
        name="rotate_keys",
    )(keys, values, key_norm_gain[None, :], positions[None, :], freq)

    half = period // 2
    across = move(kv, lambda z: (z + half if z >= half else z - half) if z < period else None)
    inside = move(
        kv, lambda z: z + half if z < half else (z - half if z < period and z % 2 == 0 else None)
    )
    beneath = move(kv, lambda z: z + 1 if period <= z < depth - 1 else None)

    query = pl.pallas_call(
        query_kernel,
        out_shape=shape((heads * rows + PAD, HEAD), jnp.bfloat16),
        in_specs=[HBM] * 6,
        out_specs=VMEM,
        scratch_shapes=[
            pltpu.VMEM((rows, heads * HEAD), jnp.bfloat16),
            pltpu.VMEM((1, HEAD), jnp.float32),
            pltpu.VMEM((rows, HEAD), jnp.float32),
            pltpu.VMEM((rows, HEAD), jnp.float32),
            pltpu.VMEM(block_mask.shape, jnp.int32),
            pltpu.VMEM((1, rows), jnp.int32),
            pltpu.SemaphoreType.DMA((6,)),
        ],
        cost_estimate=COST,
        name="rotate_queries",
    )(queries, query_norm_gain[None, :], cosine, sine, block_mask, positions[None, :])
    query_cross = swap(query)

    def number(offset):
        return (plane + offset) % period * 2 + lane

    odd = plane % 2
    numbers = [mine, mine + 1 - 2 * lane, mine, mine - 2]
    numbers += [number(0), number(4), number(-1), number(3), number(1), number(5)]
    numbers += [number(2 + 4 * odd), number(6 - 4 * odd)]
    numbers = jnp.stack(numbers).astype(jnp.int32)
    info_own = jnp.concatenate([numbers, block_mask.reshape(-1)])
    mask_cross = query_cross[heads * rows, :].astype(jnp.int32)
    info = jnp.concatenate([info_own, mask_cross])

    def attend(info, jobs, slots, queries_in, states, shards, counts, name):
        out_shape, scratch = [], []
        for job in jobs:
            sums = shape((heads * rows, 2 * HEAD), jnp.float32)
            if job["pack"]:
                scratch.append(pltpu.VMEM(sums.shape, sums.dtype))
                sums = shape((heads * rows + 2 * heads * rows // HEAD, HEAD), jnp.bfloat16)
            out_shape.append(sums)
        inputs = [info] + queries_in + states + shards
        return pl.pallas_call(
            functools.partial(
                attend_kernel,
                jobs=jobs,
                slots=slots,
                counts=counts,
                rows=rows,
                heads=heads,
                prompt=prompt,
            ),
            out_shape=out_shape,
            in_specs=[SMEM] + [VMEM] * (len(inputs) - 1),
            out_specs=[VMEM] * len(out_shape),
            scratch_shapes=scratch,
            cost_estimate=COST,
            compiler_params=PARAMS,
            name=name,
        )(*inputs)

    def job(lane, state, pack=False):
        return dict(lane=lane, state=state, pack=pack)

    near_slots = [(NEAR, True), (NEAR + 1, True)]
    (near_own,) = attend(
        info_own, [job(0, False)], near_slots[:1], [query], [], [kv], [1], "attend_near"
    )
    across, near_own = lax.optimization_barrier((across, near_own))
    first = pl.pallas_call(
        functools.partial(choose_kernel, period=period),
        out_shape=shape(kv.shape, kv.dtype),
        in_specs=[SMEM] + [VMEM] * 2,
        out_specs=VMEM,
        compiler_params=PARAMS,
        cost_estimate=pl.CostEstimate(flops=CHOOSE, bytes_accessed=1, transcendentals=0),
        name="choose_shard",
    )(numbers, inside, across)
    aside = [(z + half if z % 2 else z - half) % depth for z in range(depth)]
    second = move(first, lambda z: aside[z] if aside[z] >= period else None)
    (near_cross,) = attend(
        info, [job(1, False)], near_slots, [query_cross], [], [kv, beneath], [1, 1], "attend_near_cross"
    )
    second, near_cross = lax.optimization_barrier((second, near_cross))

    held = pl.pallas_call(
        functools.partial(hold_kernel, period=period),
        out_shape=shape((2 * 2 * rows, HEAD), jnp.bfloat16),
        in_specs=[SMEM] + [VMEM] * 3,
        out_specs=VMEM,
        compiler_params=PARAMS,
        cost_estimate=pl.CostEstimate(flops=10**10, bytes_accessed=10**8, transcendentals=0),
        name="hold_shards",
    )(numbers, kv, first, second)
    low = move(held, lambda z: z + 1 if z + 1 < depth else None)
    high = move(held, lambda z: z - 1 if not 1 <= z < half else None)
    skip = move(
        held, lambda z: None if z in (2, depth - 1) else (z + 2 if z % 2 else z - 2)
    )

    held_slots = [(HELD, False), (HELD + 1, False)]
    low_slots = [(LOW, False), (LOW + 1, False)]
    high_slots = [(HIGH, False), (HIGH + 1, False)]
    skip_slots = [(SKIP, False), (SKIP + 1, False)]
    (cross,) = attend(
        info, [job(1, True)], held_slots, [query_cross], [near_cross], [held], [2], "attend_held_cross"
    )
    (cross,) = attend(
        info,
        [job(1, True)],
        low_slots + high_slots,
        [query_cross],
        [cross],
        [low, high],
        [2, 2],
        "attend_next_cross",
    )
    (cross,) = attend(
        info, [job(1, True, True)], skip_slots, [query_cross], [cross], [skip], [2], "attend_last_cross"
    )
    other = swap(cross)
    (own,) = attend(
        info_own,
        [job(0, True)],
        held_slots + low_slots + high_slots + skip_slots + near_slots[1:],
        [query],
        [near_own],
        [held, low, high, skip, beneath],
        [2, 2, 2, 2, 1],
        "attend_own",
    )
    return pl.pallas_call(
        finish_kernel,
        out_shape=shape((rows, heads * HEAD), jnp.bfloat16),
        in_specs=[VMEM] * 2,
        out_specs=VMEM,
        compiler_params=PARAMS,
        cost_estimate=COST,
        name="finish",
    )(own, other)


def solution(mesh):
    return jax.shard_map(
        local,
        mesh=mesh,
        in_specs=(
            P(("dp", "ctx"), "tp"),
            P(("dp", "ctx"), "tp"),
            P(("dp", "ctx"), "tp"),
            P(),
            P(),
            P(("dp", "ctx")),
            P(("dp", "ctx")),
            P(("dp", "ctx"), None),
        ),
        out_specs=P(("dp", "ctx"), "tp"),
        check_vma=False,
    )
```

time: 92 us -> 74.8 us (0.81)
  the two profiles are of different devices: /device:TPU:2 before, /device:TPU:88 now
where the time goes in v2:
time: 74.8 us; the launch traced here: 74.3 us
  starting transfers between devices  28.6 us (38%)
  waiting for transfers between devices  23.7 us (32%)
  Pallas kernels  18.7 us (25%)
  local copies, waits for them, and re-layouts  2.99 us (4%)
    ppermute x7, starting transfers between devices, move(): return lax.ppermute(array, 'ctx', pairs)  23.3 us
    ppermute x2, waiting for transfers between devices, swap(): return lax.ppermute(array, 'ctx', [(c, c ^ 1) for c in range(ring)])  13.3 us
    pallas_call x6, Pallas kernels, attend(): pl.pallas_call(functools.partial(attend_kernel, jobs=jobs, slots=slots, c...  11.2 us
    ppermute x7, waiting for transfers between devices, move(): return lax.ppermute(array, 'ctx', pairs)  10.4 us
    ppermute x2, starting transfers between devices, swap(): return lax.ppermute(array, 'ctx', [(c, c ^ 1) for c in range(ring)])  5.3 us
    pallas_call x1, Pallas kernels, local(): pl.pallas_call(query_kernel, out_shape=shape((heads * rows + PAD, HEAD),...  3.21 us
    unnamed x8, local copies, waits for them, and re-layouts  1.96 us
    pallas_call x1, Pallas kernels, local(): pl.pallas_call(key_kernel, out_shape=[shape((2 * rows, HEAD), jnp.bfloat1...  1.93 us
  transfers between devices with their start and end apart: 9, of which 4 were waited for; matrix products, arithmetic and copies ran while one was open for 1% of the time, Pallas kernels for 17%

profile of v2, /device:TPU:88, one launch (start us, length us, event | category | flops | bytes accessed | tf_op | source)
XLA Modules:
  0.0 74.3 jit_solution(2109671810588821491)
XLA Ops:
  0.0 1.9 %rotate_keys.1 = (bf16[512,128]{1,0:T(8,128)(2,1)}, f32[256,128]{1,0:T(8,128)}, f32[256,128]{1,0:T(8,128)}) custom-call(bf16[256,128]{1,0:T(8,128)(2,1)} %keys.1, bf16[256,128]{1,0:T(8,128)(2,1)} %values.1, f32[1,128]{1,0:T(1,128)} %bitcast.21, s32[1,256]{1,0:T(1,128)} %bitcast.19, f32[1,128]{1,0:T(1,128)} %constant.86.clone.freq), custom_call_target="tpu_custom_call" | custom-call | flops 1 | bytes 1 | tf_op jit(solution)/shard_map/rotate_keys/pallas_call | solution.py:299
  1.9 10.9 %collective-permute-start = (bf16[512,128]{1,0:T(8,128)(2,1)}, bf16[512,128]{1,0:T(8,128)(2,1)S(1)}, u32[]{:S(2)}, u32[]{:S(2)}) collective-permute-start(bf16[512,128]{1,0:T(8,128)(2,1)} %get-tuple-element.14.refs_1_.own), channel_id=1, source_target_pairs={{0,192},{8,200},{16,208},{24,216},{32,224},{40,232},{48,240},{56,2... | collective-permute-start | bytes 393224 | tf_op jit(solution)/shard_map/ppermute | solution.py:292
  12.9 5.5 %collective-permute-start.1 = (bf16[512,128]{1,0:T(8,128)(2,1)}, bf16[512,128]{1,0:T(8,128)(2,1)S(1)}, u32[]{:S(2)}, u32[]{:S(2)}) collective-permute-start(bf16[512,128]{1,0:T(8,128)(2,1)} %get-tuple-element.14.refs_1_.own), channel_id=1, source_target_pairs={{0,64},{8,72},{16,80},{24,88},{32,96},{40,104},{48,112},{56,120},{... | collective-permute-start | bytes 393224 | tf_op jit(solution)/shard_map/ppermute | solution.py:292
  18.4 0.7 collective-permute-start.4
  19.0 3.2 %rotate_queries.1.refs_0_ = bf16[2064,128]{1,0:T(8,128)(2,1)} custom-call(bf16[256,1024]{1,0:T(8,128)(2,1)} %queries.1, f32[1,128]{1,0:T(1,128)} %bitcast.22, f32[256,128]{1,0:T(8,128)} %get-tuple-element.12.cosine, f32[256,128]{1,0:T(8,128)} %get-tuple-element.13.sine, s32[2,64]{1,0:T(2,128)} %mask.1, s32[1,256]{1,0:T(1,128)} %bitcast.20), custom_call_target="tpu_custom_call" | custom-call | flops 1 | bytes 1 | tf_op jit(solution)/shard_map/rotate_queries/pallas_call | solution.py:326
  22.4 0.8 %reshape.5 = s32[128]{0:T(128)S(1)} reshape(s32[2,64]{1,0:T(2,128)} %mask.1) | data formatting | bytes 1024 | tf_op jit(solution)/shard_map/reshape | solution.py:353
  23.2 0.1 concatenate.8.info
  23.2 2.7 %collective-permute-start.3 = (bf16[2064,128]{1,0:T(8,128)(2,1)}, bf16[2064,128]{1,0:T(8,128)(2,1)S(1)}, u32[]{:S(2)}, u32[]{:S(2)}) collective-permute-start(bf16[2064,128]{1,0:T(8,128)(2,1)} %rotate_queries.1.refs_0_), channel_id=1, source_target_pairs={{0,8},{8,0},{16,24},{24,16},{32,40},{40,32},{48,56},{56,48},{64,72... | collective-permute-start | bytes 1585160 | tf_op jit(solution)/shard_map/ppermute | solution.py:295
  25.9 0.0 copy-start
  25.9 1.0 %copy-done = bf16[2064,128]{1,0:T(8,128)(2,1)S(1)} copy-done((bf16[2064,128]{1,0:T(8,128)(2,1)S(1)}, bf16[2064,128]{1,0:T(8,128)(2,1)}, u32[]{:S(2)}) %copy-start) | copy-done | bytes 528408
  27.0 0.0 copy-start.2
  27.0 0.9 %copy-done.2 = bf16[512,128]{1,0:T(8,128)(2,1)S(1)} copy-done((bf16[512,128]{1,0:T(8,128)(2,1)S(1)}, bf16[512,128]{1,0:T(8,128)(2,1)}, u32[]{:S(2)}) %copy-start.2) | copy-done | bytes 131096
  27.9 0.7 attend_near.1.refs_1_
  28.6 0.1 stack.48.info
  28.6 0.0 copy-start.3
  28.7 0.0 collective-permute-done.across
  28.7 0.0 collective-permute-done.1.inside
  28.7 0.6 choose_shard.1.opposite
  29.3 1.3 %collective-permute-start.2 = (bf16[512,128]{1,0:T(8,128)(2,1)S(1)}, bf16[512,128]{1,0:T(8,128)(2,1)S(1)}, u32[]{:S(2)}, u32[]{:S(2)}) collective-permute-start(bf16[512,128]{1,0:T(8,128)(2,1)S(1)} %choose_shard.1.opposite), channel_id=1, source_target_pairs={{0,192},{8,200},{32,224},{40,232},{80,144},{88,152},{112,176},{120... | collective-permute-start | bytes 393224 | tf_op jit(solution)/shard_map/ppermute | solution.py:292
  30.6 8.0 %collective-permute-done.3.refs_0_ = bf16[2064,128]{1,0:T(8,128)(2,1)S(1)} collective-permute-done((bf16[2064,128]{1,0:T(8,128)(2,1)}, bf16[2064,128]{1,0:T(8,128)(2,1)S(1)}, u32[]{:S(2)}, u32[]{:S(2)}) %collective-permute-start.3) | collective-permute-done | bytes 528416 | tf_op jit(solution)/shard_map/ppermute | solution.py:295
  38.5 0.1 concatenate.9.info
  38.6 0.0 collective-permute-done.4.refs_2_.refs_6_
  38.6 0.0 copy-done.3
  38.7 0.7 attend_near_cross.1.refs_1_
  39.4 0.0 collective-permute-done.2.second
  39.4 0.6 hold_shards.1.refs_2_
  40.0 2.9 %collective-permute-start.5 = (bf16[1024,128]{1,0:T(8,128)(2,1)S(1)}, bf16[1024,128]{1,0:T(8,128)(2,1)S(1)}, u32[]{:S(2)}, u32[]{:S(2)}) collective-permute-start(bf16[1024,128]{1,0:T(8,128)(2,1)S(1)} %hold_shards.1.refs_2_), channel_id=1, source_target_pairs={{0,16},{8,24},{16,32},{24,40},{32,48},{40,56},{48,64},{56,72},{64,... | collective-permute-start | bytes 786440 | tf_op jit(solution)/shard_map/ppermute | solution.py:292
  42.9 0.7 collective-permute-start.6
  43.6 1.3 %collective-permute-start.7 = (bf16[1024,128]{1,0:T(8,128)(2,1)S(1)}, bf16[1024,128]{1,0:T(8,128)(2,1)S(1)}, u32[]{:S(2)}, u32[]{:S(2)}) collective-permute-start(bf16[1024,128]{1,0:T(8,128)(2,1)S(1)} %hold_shards.1.refs_2_), channel_id=1, source_target_pairs={{0,224},{8,232},{16,48},{24,56},{48,80},{56,88},{64,32},{72,40},{8... | collective-permute-start | bytes 786440 | tf_op jit(solution)/shard_map/ppermute | solution.py:292
  44.9 0.7 attend_held_cross.1.refs_1_
  45.6 3.9 %collective-permute-done.5.refs_3_.refs_2_ = bf16[1024,128]{1,0:T(8,128)(2,1)S(1)} collective-permute-done((bf16[1024,128]{1,0:T(8,128)(2,1)S(1)}, bf16[1024,128]{1,0:T(8,128)(2,1)S(1)}, u32[]{:S(2)}, u32[]{:S(2)}) %collective-permute-start.5) | collective-permute-done | bytes 262176 | tf_op jit(solution)/shard_map/ppermute | solution.py:292
  49.6 0.0 collective-permute-done.6.refs_4_.refs_3_
  49.6 2.3 %attend_next_cross.1.refs_1_ = f32[2048,256]{1,0:T(8,128)S(1)} custom-call(s32[268]{0:T(512)S(1)} %concatenate.9.info, bf16[2064,128]{1,0:T(8,128)(2,1)S(1)} %collective-permute-done.3.refs_0_, f32[2048,256]{1,0:T(8,128)S(1)} %attend_held_cross.1.refs_1_, bf16[1024,128]{1,0:T(8,128)(2,1)S(1)} %collective-permute-done.5.refs_3_.refs_2_, ...), custom_call_target="tpu_custom_call" | custom-call | flops 1 | bytes 1 | tf_op jit(solution)/shard_map/attend_next_cross/pallas_call | solution.py:366
  51.8 0.0 copy-start.1
  51.8 6.5 %collective-permute-done.7.refs_5_.refs_2_ = bf16[1024,128]{1,0:T(8,128)(2,1)S(1)} collective-permute-done((bf16[1024,128]{1,0:T(8,128)(2,1)S(1)}, bf16[1024,128]{1,0:T(8,128)(2,1)S(1)}, u32[]{:S(2)}, u32[]{:S(2)}) %collective-permute-start.7) | collective-permute-done | bytes 262176 | tf_op jit(solution)/shard_map/ppermute | solution.py:292
  58.4 2.0 %attend_last_cross.1 = bf16[2080,128]{1,0:T(8,128)(2,1)S(1)} custom-call(s32[268]{0:T(512)S(1)} %concatenate.9.info, bf16[2064,128]{1,0:T(8,128)(2,1)S(1)} %collective-permute-done.3.refs_0_, f32[2048,256]{1,0:T(8,128)S(1)} %attend_next_cross.1.refs_1_, bf16[1024,128]{1,0:T(8,128)(2,1)S(1)} %collective-permute-done.7.refs_5_.refs_2_), custom_call_target="tpu_custom_call" | custom-call | flops 1 | bytes 1 | tf_op jit(solution)/shard_map/attend_last_cross/pallas_call | solution.py:366
  60.4 2.7 %collective-permute-start.8 = (bf16[2080,128]{1,0:T(8,128)(2,1)S(1)}, bf16[2080,128]{1,0:T(8,128)(2,1)S(1)}, u32[]{:S(2)}, u32[]{:S(2)}) collective-permute-start(bf16[2080,128]{1,0:T(8,128)(2,1)S(1)} %attend_last_cross.1), channel_id=1, source_target_pairs={{0,8},{8,0},{16,24},{24,16},{32,40},{40,32},{48,56},{56,48},{64,72... | collective-permute-start | bytes 1597448 | tf_op jit(solution)/shard_map/ppermute | solution.py:295
  63.1 0.0 copy-done.1
  63.1 4.8 %attend_own.1.own = f32[2048,256]{1,0:T(8,128)S(1)} custom-call(s32[140]{0:T(256)S(1)} %concatenate.8.info, bf16[2064,128]{1,0:T(8,128)(2,1)S(1)} %copy-done.1, f32[2048,256]{1,0:T(8,128)S(1)} %attend_near.1.refs_1_, bf16[1024,128]{1,0:T(8,128)(2,1)S(1)} %hold_shards.1.refs_2_, bf16[1024,128]{1,0:T(8,128)(2,1)S(1)} %collective-permute-done.5.refs_3_.refs_2_, ...), custom_call_target="tpu_custom_call" | custom-call | flops 1 | bytes 1 | tf_op jit(solution)/shard_map/attend_own/pallas_call | solution.py:366
  67.9 5.3 %collective-permute-done.8.other = bf16[2080,128]{1,0:T(8,128)(2,1)S(1)} collective-permute-done((bf16[2080,128]{1,0:T(8,128)(2,1)S(1)}, bf16[2080,128]{1,0:T(8,128)(2,1)S(1)}, u32[]{:S(2)}, u32[]{:S(2)}) %collective-permute-start.8) | collective-permute-done | bytes 532512 | tf_op jit(solution)/shard_map/ppermute | solution.py:295
  73.2 1.2 %finish.1 = bf16[256,1024]{1,0:T(8,128)(2,1)} custom-call(f32[2048,256]{1,0:T(8,128)S(1)} %attend_own.1.own, bf16[2080,128]{1,0:T(8,128)(2,1)S(1)} %collective-permute-done.8.other), custom_call_target="tpu_custom_call" | custom-call | flops 1 | bytes 1 | tf_op jit(solution)/shard_map/finish/pallas_call | solution.py:455
  (1 shorter events, 0.0 us)
Async XLA Ops:
  1.9 26.7 %collective-permute-start = (bf16[512,128]{1,0:T(8,128)(2,1)}, bf16[512,128]{1,0:T(8,128)(2,1)S(1)}, u32[]{:S(2)}, u32[]{:S(2)}) collective-permute-start(bf16[512,128]{1,0:T(8,128)(2,1)} %get-tuple-element.14.refs_1_.own), channel_id=1, source_target_pairs={{0,192},{8,200},{16,208},{24,216},{32,224},{40,232},{48,240},{56,2... | collective-permute-start | bytes 393224 | tf_op jit(solution)/shard_map/ppermute | solution.py:292
  12.9 15.8 %collective-permute-start.1 = (bf16[512,128]{1,0:T(8,128)(2,1)}, bf16[512,128]{1,0:T(8,128)(2,1)S(1)}, u32[]{:S(2)}, u32[]{:S(2)}) collective-permute-start(bf16[512,128]{1,0:T(8,128)(2,1)} %get-tuple-element.14.refs_1_.own), channel_id=1, source_target_pairs={{0,64},{8,72},{16,80},{24,88},{32,96},{40,104},{48,112},{56,120},{... | collective-permute-start | bytes 393224 | tf_op jit(solution)/shard_map/ppermute | solution.py:292
  18.4 20.3 %collective-permute-start.4 = (bf16[512,128]{1,0:T(8,128)(2,1)}, bf16[512,128]{1,0:T(8,128)(2,1)S(1)}, u32[]{:S(2)}, u32[]{:S(2)}) collective-permute-start(bf16[512,128]{1,0:T(8,128)(2,1)} %get-tuple-element.14.refs_1_.own), channel_id=1, source_target_pairs={{128,144},{136,152},{144,160},{152,168},{160,176},{168,184},{176,1... | collective-permute-start | bytes 393224 | tf_op jit(solution)/shard_map/ppermute | solution.py:292
  23.2 15.3 %collective-permute-start.3 = (bf16[2064,128]{1,0:T(8,128)(2,1)}, bf16[2064,128]{1,0:T(8,128)(2,1)S(1)}, u32[]{:S(2)}, u32[]{:S(2)}) collective-permute-start(bf16[2064,128]{1,0:T(8,128)(2,1)} %rotate_queries.1.refs_0_), channel_id=1, source_target_pairs={{0,8},{8,0},{16,24},{24,16},{32,40},{40,32},{48,56},{56,48},{64,72... | collective-permute-start | bytes 1585160 | tf_op jit(solution)/shard_map/ppermute | solution.py:295
  25.9 1.1 %copy-start = (bf16[2064,128]{1,0:T(8,128)(2,1)S(1)}, bf16[2064,128]{1,0:T(8,128)(2,1)}, u32[]{:S(2)}) copy-start(bf16[2064,128]{1,0:T(8,128)(2,1)} %rotate_queries.1.refs_0_) | copy-start | bytes 1585156
  27.0 0.9 %copy-start.2 = (bf16[512,128]{1,0:T(8,128)(2,1)S(1)}, bf16[512,128]{1,0:T(8,128)(2,1)}, u32[]{:S(2)}) copy-start(bf16[512,128]{1,0:T(8,128)(2,1)} %get-tuple-element.14.refs_1_.own) | copy-start | bytes 393220
  28.6 10.0 %copy-start.3 = (bf16[512,128]{1,0:T(8,128)(2,1)S(1)}, bf16[512,128]{1,0:T(8,128)(2,1)}, u32[]{:S(2)}) copy-start(bf16[512,128]{1,0:T(8,128)(2,1)} %get-tuple-element.14.refs_1_.own) | copy-start | bytes 393220
  29.3 10.1 %collective-permute-start.2 = (bf16[512,128]{1,0:T(8,128)(2,1)S(1)}, bf16[512,128]{1,0:T(8,128)(2,1)S(1)}, u32[]{:S(2)}, u32[]{:S(2)}) collective-permute-start(bf16[512,128]{1,0:T(8,128)(2,1)S(1)} %choose_shard.1.opposite), channel_id=1, source_target_pairs={{0,192},{8,200},{32,224},{40,232},{80,144},{88,152},{112,176},{120... | collective-permute-start | bytes 393224 | tf_op jit(solution)/shard_map/ppermute | solution.py:292
  40.0 9.6 %collective-permute-start.5 = (bf16[1024,128]{1,0:T(8,128)(2,1)S(1)}, bf16[1024,128]{1,0:T(8,128)(2,1)S(1)}, u32[]{:S(2)}, u32[]{:S(2)}) collective-permute-start(bf16[1024,128]{1,0:T(8,128)(2,1)S(1)} %hold_shards.1.refs_2_), channel_id=1, source_target_pairs={{0,16},{8,24},{16,32},{24,40},{32,48},{40,56},{48,64},{56,72},{64,... | collective-permute-start | bytes 786440 | tf_op jit(solution)/shard_map/ppermute | solution.py:292
  42.9 6.7 %collective-permute-start.6 = (bf16[1024,128]{1,0:T(8,128)(2,1)S(1)}, bf16[1024,128]{1,0:T(8,128)(2,1)S(1)}, u32[]{:S(2)}, u32[]{:S(2)}) collective-permute-start(bf16[1024,128]{1,0:T(8,128)(2,1)S(1)} %hold_shards.1.refs_2_), channel_id=1, source_target_pairs={{0,240},{8,248},{64,48},{72,56},{80,64},{88,72},{96,80},{104,88},{... | collective-permute-start | bytes 786440 | tf_op jit(solution)/shard_map/ppermute | solution.py:292
  43.6 14.8 %collective-permute-start.7 = (bf16[1024,128]{1,0:T(8,128)(2,1)S(1)}, bf16[1024,128]{1,0:T(8,128)(2,1)S(1)}, u32[]{:S(2)}, u32[]{:S(2)}) collective-permute-start(bf16[1024,128]{1,0:T(8,128)(2,1)S(1)} %hold_shards.1.refs_2_), channel_id=1, source_target_pairs={{0,224},{8,232},{16,48},{24,56},{48,80},{56,88},{64,32},{72,40},{8... | collective-permute-start | bytes 786440 | tf_op jit(solution)/shard_map/ppermute | solution.py:292
  51.8 11.2 %copy-start.1 = (bf16[2064,128]{1,0:T(8,128)(2,1)S(1)}, bf16[2064,128]{1,0:T(8,128)(2,1)}, u32[]{:S(2)}) copy-start(bf16[2064,128]{1,0:T(8,128)(2,1)} %rotate_queries.1.refs_0_) | copy-start | bytes 1585156
  60.4 12.8 %collective-permute-start.8 = (bf16[2080,128]{1,0:T(8,128)(2,1)S(1)}, bf16[2080,128]{1,0:T(8,128)(2,1)S(1)}, u32[]{:S(2)}, u32[]{:S(2)}) collective-permute-start(bf16[2080,128]{1,0:T(8,128)(2,1)S(1)} %attend_last_cross.1), channel_id=1, source_target_pairs={{0,8},{8,0},{16,24},{24,16},{32,40},{40,32},{48,56},{56,48},{64,72... | collective-permute-start | bytes 1597448 | tf_op jit(solution)/shard_map/ppermute | solution.py:295

commit v3 on v2

--- a/solution.py
+++ b/solution.py
@@ -135,7 +135,7 @@
     held[size:, :] = opposite[...]
 
 
-def attend_kernel(info, *refs, jobs, slots, counts, rows, heads, prompt):
+def attend_kernel(info, *refs, jobs, slots, counts, rows, heads, span, prompt):
     refs = list(refs)
     queries = [refs.pop(0) for _ in jobs]
     states = [refs.pop(0) if job["state"] else None for job in jobs]
@@ -144,6 +144,7 @@
         ref = refs.pop(0)
         shards += [(ref, part * 2 * rows) for part in range(count)]
     half = rows // 2
+    begin, end = span
     scale = HEAD**-0.5 * math.log2(math.e)
     ones = jnp.ones((rows, HEAD), jnp.bfloat16)
 
@@ -184,12 +185,12 @@
                 early.append((shard, number, any_seen, all_seen))
 
         def add(shard, mask, query=query, total=total):
-            @pl.loop(0, heads // 4)
+            @pl.loop(0, (end - begin) // 4)
             def _(group):
                 for inner in range(4):
                     head = group * 4 + inner
                     at = pl.ds(pl.multiple_of(head * rows, rows), rows)
-                    total[at, :] += partial(query, head, shard, mask)
+                    total[at, :] += partial(query, begin + head, shard, mask)
 
         def add_masked(shard, number, near, add=add, block=block, query=query, mine=mine):
             row = lax.broadcasted_iota(jnp.int32, (rows, rows), 0)
@@ -210,16 +211,15 @@
             add(shard, mask)
 
         def together(query=query, state=state, total=total, early=early):
-            for head in range(heads):
-                at = pl.ds(head * rows, rows)
-                sums = None if state is None else state[at, :]
+            for head in range(begin, end):
+                sums = None if state is None else state[head * rows : (head + 1) * rows, :]
                 for shard, *_ in early:
                     new = partial(query, head, shard, None)
                     sums = new if sums is None else sums + new
-                total[at, :] = sums
+                total[(head - begin) * rows : (head - begin + 1) * rows, :] = sums
 
         def one_by_one(state=state, total=total, early=early, add=add, add_masked=add_masked):
-            total[...] = jnp.zeros_like(total) if state is None else state[...]
+            total[...] = jnp.zeros_like(total) if state is None else state[begin * rows : end * rows, :]
             for shard, number, any_seen, all_seen in early:
                 pl.when(all_seen)(functools.partial(add, shard, None))
                 pl.when(any_seen & jnp.logical_not(all_seen))(
@@ -236,42 +236,44 @@
             pl.when(any_seen)(functools.partial(add_masked, shard, number, True))
 
         if job["pack"]:
+            count = end - begin
             at_lane = lax.broadcasted_iota(jnp.int32, (rows, HEAD), 1)
             packed = jnp.zeros((rows, HEAD), jnp.float32)
-            for head in range(heads):
+            for head in range(count):
                 at = pl.ds(head * rows, rows)
                 out[at, :] = total[at, :HEAD].astype(out.dtype)
                 whole = total[at, HEAD:]
                 high = whole.astype(jnp.bfloat16).astype(jnp.float32)
                 packed = jnp.where(at_lane == head, high, packed)
-                packed = jnp.where(at_lane == heads + head, whole - high, packed)
-            turned = packed.T[: 2 * heads, :].astype(out.dtype)
-            for part in range(rows // HEAD):
-                at = pl.ds(heads * rows + part * 2 * heads, 2 * heads)
-                out[at, :] = turned[:, part * HEAD : (part + 1) * HEAD]
-
-
-def finish_kernel(own, other, out):
+                packed = jnp.where(at_lane == count + head, whole - high, packed)
+            turned = packed.T[: 2 * count, :]
+            turned = [turned[:, at : at + HEAD] for at in range(0, rows, HEAD)]
+            out[count * rows :, :] = jnp.concatenate(turned, axis=0).astype(out.dtype)
+
+
+def finish_kernel(own, *refs):
+    *others, out = refs
     rows = out.shape[0]
-    heads = out.shape[1] // HEAD
-    base = heads * rows
-    packed = jnp.concatenate(
-        [other[base + p * 2 * heads : base + (p + 1) * 2 * heads, :] for p in range(rows // HEAD)],
-        axis=1,
-    )
-    source = lax.broadcasted_iota(jnp.int32, (2 * heads, HEAD), 0)
-    for head in range(heads):
-        at = slice(head * rows, (head + 1) * rows)
-        pick = jnp.where((source == head) | (source == heads + head), 1.0, 0.0)
-        total = lax.dot_general(
-            packed,
-            pick.astype(jnp.bfloat16),
-            (((0,), (0,)), ((), ())),
-            preferred_element_type=jnp.float32,
-        )
-        total = total + own[at, HEAD:]
-        value = own[at, :HEAD] + other[at, :].astype(jnp.float32)
-        out[:, head * HEAD : (head + 1) * HEAD] = (value / total).astype(out.dtype)
+    count = out.shape[1] // HEAD // len(others)
+    source = lax.broadcasted_iota(jnp.int32, (2 * count, HEAD), 0)
+    for part, other in enumerate(others):
+        packed = other[count * rows :, :].astype(jnp.float32)
+        packed = [packed[at : at + 2 * count, :] for at in range(0, packed.shape[0], 2 * count)]
+        packed = jnp.concatenate(packed, axis=1).astype(jnp.bfloat16)
+        for head in range(count):
+            at = slice(head * rows, (head + 1) * rows)
+            own_at = slice((part * count + head) * rows, (part * count + head + 1) * rows)
+            pick = jnp.where((source == head) | (source == count + head), 1.0, 0.0)
+            total = lax.dot_general(
+                packed,
+                pick.astype(jnp.bfloat16),
+                (((0,), (0,)), ((), ())),
+                preferred_element_type=jnp.float32,
+            )
+            total = total + own[own_at, HEAD:]
+            value = own[own_at, :HEAD] + other[at, :].astype(jnp.float32)
+            lanes = slice((part * count + head) * HEAD, (part * count + head + 1) * HEAD)
+            out[:, lanes] = (value / total).astype(out.dtype)
 
 
 def local(
@@ -354,13 +356,14 @@
     mask_cross = query_cross[heads * rows, :].astype(jnp.int32)
     info = jnp.concatenate([info_own, mask_cross])
 
-    def attend(info, jobs, slots, queries_in, states, shards, counts, name):
+    def attend(info, jobs, slots, queries_in, states, shards, counts, name, span=(0, heads)):
         out_shape, scratch = [], []
+        size = (span[1] - span[0]) * rows
         for job in jobs:
-            sums = shape((heads * rows, 2 * HEAD), jnp.float32)
+            sums = shape((size, 2 * HEAD), jnp.float32)
             if job["pack"]:
                 scratch.append(pltpu.VMEM(sums.shape, sums.dtype))
-                sums = shape((heads * rows + 2 * heads * rows // HEAD, HEAD), jnp.bfloat16)
+                sums = shape((size + 2 * size // HEAD, HEAD), jnp.bfloat16)
             out_shape.append(sums)
         inputs = [info] + queries_in + states + shards
         return pl.pallas_call(
@@ -371,6 +374,7 @@
                 counts=counts,
                 rows=rows,
                 heads=heads,
+                span=span,
                 prompt=prompt,
             ),
             out_shape=out_shape,
@@ -386,8 +390,9 @@
         return dict(lane=lane, state=state, pack=pack)
 
     near_slots = [(NEAR, True), (NEAR + 1, True)]
+    inside, query_own = lax.optimization_barrier((inside, query))
     (near_own,) = attend(
-        info_own, [job(0, False)], near_slots[:1], [query], [], [kv], [1], "attend_near"
+        info_own, [job(0, False)], near_slots[:1], [query_own], [], [kv], [1], "attend_near"
     )
     across, near_own = lax.optimization_barrier((across, near_own))
     first = pl.pallas_call(
@@ -431,15 +436,15 @@
     (cross,) = attend(
         info,
         [job(1, True)],
-        low_slots + high_slots,
+        skip_slots + low_slots,
         [query_cross],
         [cross],
-        [low, high],
+        [skip, low],
         [2, 2],
         "attend_next_cross",
     )
     (cross,) = attend(
-        info, [job(1, True, True)], skip_slots, [query_cross], [cross], [skip], [2], "attend_last_cross"
+        info, [job(1, True, True)], high_slots, [query_cross], [cross], [high], [2], "attend_last_cross"
     )
     other = swap(cross)
     (own,) = attend(

time: 74.8 us -> 73.5 us (0.983)
  the two profiles are of different devices: /device:TPU:88 before, /device:TPU:326 now
where the time goes in v3:
time: 73.5 us; the launch traced here: 73.1 us
  starting transfers between devices  25.1 us (34%)
  Pallas kernels  24.2 us (33%)
  waiting for transfers between devices  20.4 us (28%)
  local copies, waits for them, and re-layouts  2.98 us (4%)
    ppermute x7, starting transfers between devices, move(): return lax.ppermute(array, 'ctx', pairs)  19.2 us
    pallas_call x6, Pallas kernels, attend(): pl.pallas_call(functools.partial(attend_kernel, jobs=jobs, slots=slots, c...  16.7 us
    ppermute x2, waiting for transfers between devices, swap(): return lax.ppermute(array, 'ctx', [(c, c ^ 1) for c in range(ring)])  12.9 us
    ppermute x7, waiting for transfers between devices, move(): return lax.ppermute(array, 'ctx', pairs)  7.48 us
    ppermute x2, starting transfers between devices, swap(): return lax.ppermute(array, 'ctx', [(c, c ^ 1) for c in range(ring)])  5.9 us
    pallas_call x1, Pallas kernels, local(): pl.pallas_call(query_kernel, out_shape=shape((heads * rows + PAD, HEAD),...  3.21 us
    unnamed x8, local copies, waits for them, and re-layouts  1.95 us
    pallas_call x1, Pallas kernels, local(): pl.pallas_call(key_kernel, out_shape=[shape((2 * rows, HEAD), jnp.bfloat1...  1.93 us
  transfers between devices with their start and end apart: 9, of which 6 were waited for; matrix products, arithmetic and copies ran while one was open for 1% of the time, Pallas kernels for 25%

profile of v3, /device:TPU:326, one launch (start us, length us, event | category | flops | bytes accessed | tf_op | source)
XLA Modules:
  0.0 73.1 jit_solution(16397259506270292824)
XLA Ops:
  0.0 1.9 %rotate_keys.1 = (bf16[512,128]{1,0:T(8,128)(2,1)}, f32[256,128]{1,0:T(8,128)}, f32[256,128]{1,0:T(8,128)}) custom-call(bf16[256,128]{1,0:T(8,128)(2,1)} %keys.1, bf16[256,128]{1,0:T(8,128)(2,1)} %values.1, f32[1,128]{1,0:T(1,128)} %bitcast.21, s32[1,256]{1,0:T(1,128)} %bitcast.19, f32[1,128]{1,0:T(1,128)} %constant.86.clone.freq), custom_call_target="tpu_custom_call" | custom-call | flops 1 | bytes 1 | tf_op jit(solution)/shard_map/rotate_keys/pallas_call | solution.py:301
  1.9 0.7 collective-permute-start.1
  2.6 1.3 %collective-permute-start = (bf16[512,128]{1,0:T(8,128)(2,1)}, bf16[512,128]{1,0:T(8,128)(2,1)S(1)}, u32[]{:S(2)}, u32[]{:S(2)}) collective-permute-start(bf16[512,128]{1,0:T(8,128)(2,1)} %get-tuple-element.16.refs_1_.own), channel_id=1, source_target_pairs={{0,192},{8,200},{16,208},{24,216},{32,224},{40,232},{48,240},{56,2... | collective-permute-start | bytes 393224 | tf_op jit(solution)/shard_map/ppermute | solution.py:294
  3.9 2.9 %collective-permute-start.4 = (bf16[512,128]{1,0:T(8,128)(2,1)}, bf16[512,128]{1,0:T(8,128)(2,1)S(1)}, u32[]{:S(2)}, u32[]{:S(2)}) collective-permute-start(bf16[512,128]{1,0:T(8,128)(2,1)} %get-tuple-element.16.refs_1_.own), channel_id=1, source_target_pairs={{128,144},{136,152},{144,160},{152,168},{160,176},{168,184},{176,1... | collective-permute-start | bytes 393224 | tf_op jit(solution)/shard_map/ppermute | solution.py:294
  6.8 3.2 %rotate_queries.1.refs_0_ = bf16[2064,128]{1,0:T(8,128)(2,1)} custom-call(bf16[256,1024]{1,0:T(8,128)(2,1)} %queries.1, f32[1,128]{1,0:T(1,128)} %bitcast.22, f32[256,128]{1,0:T(8,128)} %get-tuple-element.14.cosine, f32[256,128]{1,0:T(8,128)} %get-tuple-element.15.sine, s32[2,64]{1,0:T(2,128)} %mask.1, s32[1,256]{1,0:T(1,128)} %bitcast.20), custom_call_target="tpu_custom_call" | custom-call | flops 1 | bytes 1 | tf_op jit(solution)/shard_map/rotate_queries/pallas_call | solution.py:328
  10.1 3.5 %collective-permute-start.3 = (bf16[2064,128]{1,0:T(8,128)(2,1)}, bf16[2064,128]{1,0:T(8,128)(2,1)S(1)}, u32[]{:S(2)}, u32[]{:S(2)}) collective-permute-start(bf16[2064,128]{1,0:T(8,128)(2,1)} %rotate_queries.1.refs_0_), channel_id=1, source_target_pairs={{0,8},{8,0},{16,24},{24,16},{32,40},{40,32},{48,56},{56,48},{64,72... | collective-permute-start | bytes 1585160 | tf_op jit(solution)/shard_map/ppermute | solution.py:297
  13.7 0.8 %reshape.5 = s32[128]{0:T(128)S(1)} reshape(s32[2,64]{1,0:T(2,128)} %mask.1) | data formatting | bytes 1024 | tf_op jit(solution)/shard_map/reshape | solution.py:355
  14.5 0.1 stack.48.info
  14.5 0.1 concatenate.8.info
  14.6 0.0 collective-permute-done.1.inside
  14.7 0.0 copy-start
  14.7 1.0 %copy-done = bf16[2064,128]{1,0:T(8,128)(2,1)S(1)} copy-done((bf16[2064,128]{1,0:T(8,128)(2,1)S(1)}, bf16[2064,128]{1,0:T(8,128)(2,1)}, u32[]{:S(2)}) %copy-start) | copy-done | bytes 528408
  15.7 0.0 copy-start.2
  15.7 0.9 %copy-done.2 = bf16[512,128]{1,0:T(8,128)(2,1)S(1)} copy-done((bf16[512,128]{1,0:T(8,128)(2,1)S(1)}, bf16[512,128]{1,0:T(8,128)(2,1)}, u32[]{:S(2)}) %copy-start.2) | copy-done | bytes 131096
  16.6 1.9 %attend_near.1.refs_1_ = f32[2048,256]{1,0:T(8,128)S(1)} custom-call(s32[140]{0:T(256)S(1)} %concatenate.8.info, bf16[2064,128]{1,0:T(8,128)(2,1)S(1)} %copy-done, bf16[512,128]{1,0:T(8,128)(2,1)S(1)} %copy-done.2), custom_call_target="tpu_custom_call" | custom-call | flops 1 | bytes 1 | tf_op jit(solution)/shard_map/attend_near/pallas_call | solution.py:369
  18.5 0.0 copy-start.3
  18.5 0.0 collective-permute-done.across
  18.5 0.6 choose_shard.1.opposite
  19.1 1.3 %collective-permute-start.2 = (bf16[512,128]{1,0:T(8,128)(2,1)S(1)}, bf16[512,128]{1,0:T(8,128)(2,1)S(1)}, u32[]{:S(2)}, u32[]{:S(2)}) collective-permute-start(bf16[512,128]{1,0:T(8,128)(2,1)S(1)} %choose_shard.1.opposite), channel_id=1, source_target_pairs={{0,192},{8,200},{32,224},{40,232},{80,144},{88,152},{112,176},{120... | collective-permute-start | bytes 393224 | tf_op jit(solution)/shard_map/ppermute | solution.py:294
  20.4 5.3 %collective-permute-done.3.refs_0_ = bf16[2064,128]{1,0:T(8,128)(2,1)S(1)} collective-permute-done((bf16[2064,128]{1,0:T(8,128)(2,1)}, bf16[2064,128]{1,0:T(8,128)(2,1)S(1)}, u32[]{:S(2)}, u32[]{:S(2)}) %collective-permute-start.3) | collective-permute-done | bytes 528416 | tf_op jit(solution)/shard_map/ppermute | solution.py:297
  25.6 0.1 concatenate.9.info
  25.7 0.0 collective-permute-done.4.refs_2_.refs_6_
  25.8 0.0 copy-done.3
  25.8 1.9 %attend_near_cross.1.refs_1_ = f32[2048,256]{1,0:T(8,128)S(1)} custom-call(s32[268]{0:T(512)S(1)} %concatenate.9.info, bf16[2064,128]{1,0:T(8,128)(2,1)S(1)} %collective-permute-done.3.refs_0_, bf16[512,128]{1,0:T(8,128)(2,1)S(1)} %copy-done.3, bf16[512,128]{1,0:T(8,128)(2,1)S(1)} %collective-permute-done.4.refs_2_.refs_6_), custom_call_target="tpu_custom_call" | custom-call | flops 1 | bytes 1 | tf_op jit(solution)/shard_map/attend_near_cross/pallas_call | solution.py:369
  27.6 2.2 %collective-permute-done.2.second = bf16[512,128]{1,0:T(8,128)(2,1)S(1)} collective-permute-done((bf16[512,128]{1,0:T(8,128)(2,1)S(1)}, bf16[512,128]{1,0:T(8,128)(2,1)S(1)}, u32[]{:S(2)}, u32[]{:S(2)}) %collective-permute-start.2) | collective-permute-done | bytes 131104 | tf_op jit(solution)/shard_map/ppermute | solution.py:294
  29.9 0.6 hold_shards.1.refs_2_
  30.5 6.3 %collective-permute-start.5 = (bf16[1024,128]{1,0:T(8,128)(2,1)S(1)}, bf16[1024,128]{1,0:T(8,128)(2,1)S(1)}, u32[]{:S(2)}, u32[]{:S(2)}) collective-permute-start(bf16[1024,128]{1,0:T(8,128)(2,1)S(1)} %hold_shards.1.refs_2_), channel_id=1, source_target_pairs={{0,16},{8,24},{16,32},{24,40},{32,48},{40,56},{48,64},{56,72},{64,... | collective-permute-start | bytes 786440 | tf_op jit(solution)/shard_map/ppermute | solution.py:294
  36.8 2.7 %collective-permute-start.7 = (bf16[1024,128]{1,0:T(8,128)(2,1)S(1)}, bf16[1024,128]{1,0:T(8,128)(2,1)S(1)}, u32[]{:S(2)}, u32[]{:S(2)}) collective-permute-start(bf16[1024,128]{1,0:T(8,128)(2,1)S(1)} %hold_shards.1.refs_2_), channel_id=1, source_target_pairs={{0,224},{8,232},{16,48},{24,56},{48,80},{56,88},{64,32},{72,40},{8... | collective-permute-start | bytes 786440 | tf_op jit(solution)/shard_map/ppermute | solution.py:294
  39.4 4.0 %collective-permute-start.6 = (bf16[1024,128]{1,0:T(8,128)(2,1)S(1)}, bf16[1024,128]{1,0:T(8,128)(2,1)S(1)}, u32[]{:S(2)}, u32[]{:S(2)}) collective-permute-start(bf16[1024,128]{1,0:T(8,128)(2,1)S(1)} %hold_shards.1.refs_2_), channel_id=1, source_target_pairs={{0,240},{8,248},{64,48},{72,56},{80,64},{88,72},{96,80},{104,88},{... | collective-permute-start | bytes 786440 | tf_op jit(solution)/shard_map/ppermute | solution.py:294
  43.5 2.0 %attend_held_cross.1.refs_1_ = f32[2048,256]{1,0:T(8,128)S(1)} custom-call(s32[268]{0:T(512)S(1)} %concatenate.9.info, bf16[2064,128]{1,0:T(8,128)(2,1)S(1)} %collective-permute-done.3.refs_0_, f32[2048,256]{1,0:T(8,128)S(1)} %attend_near_cross.1.refs_1_, bf16[1024,128]{1,0:T(8,128)(2,1)S(1)} %hold_shards.1.refs_2_), custom_call_target="tpu_custom_call" | custom-call | flops 1 | bytes 1 | tf_op jit(solution)/shard_map/attend_held_cross/pallas_call | solution.py:369
  45.4 2.5 %collective-permute-done.5.refs_3_ = bf16[1024,128]{1,0:T(8,128)(2,1)S(1)} collective-permute-done((bf16[1024,128]{1,0:T(8,128)(2,1)S(1)}, bf16[1024,128]{1,0:T(8,128)(2,1)S(1)}, u32[]{:S(2)}, u32[]{:S(2)}) %collective-permute-start.5) | collective-permute-done | bytes 262176 | tf_op jit(solution)/shard_map/ppermute | solution.py:294
  47.9 2.1 %collective-permute-done.7.refs_5_.refs_2_ = bf16[1024,128]{1,0:T(8,128)(2,1)S(1)} collective-permute-done((bf16[1024,128]{1,0:T(8,128)(2,1)S(1)}, bf16[1024,128]{1,0:T(8,128)(2,1)S(1)}, u32[]{:S(2)}, u32[]{:S(2)}) %collective-permute-start.7) | collective-permute-done | bytes 262176 | tf_op jit(solution)/shard_map/ppermute | solution.py:294
  50.1 3.3 %attend_next_cross.1.refs_1_ = f32[2048,256]{1,0:T(8,128)S(1)} custom-call(s32[268]{0:T(512)S(1)} %concatenate.9.info, bf16[2064,128]{1,0:T(8,128)(2,1)S(1)} %collective-permute-done.3.refs_0_, f32[2048,256]{1,0:T(8,128)S(1)} %attend_held_cross.1.refs_1_, bf16[1024,128]{1,0:T(8,128)(2,1)S(1)} %collective-permute-done.7.refs_5_.refs_2_, ...), custom_call_target="tpu_custom_call" | custom-call | flops 1 | bytes 1 | tf_op jit(solution)/shard_map/attend_next_cross/pallas_call | solution.py:369
  53.4 0.0 copy-start.1
  53.4 0.6 collective-permute-done.6.refs_4_.refs_2_
  54.0 2.2 %attend_last_cross.1 = bf16[2080,128]{1,0:T(8,128)(2,1)S(1)} custom-call(s32[268]{0:T(512)S(1)} %concatenate.9.info, bf16[2064,128]{1,0:T(8,128)(2,1)S(1)} %collective-permute-done.3.refs_0_, f32[2048,256]{1,0:T(8,128)S(1)} %attend_next_cross.1.refs_1_, bf16[1024,128]{1,0:T(8,128)(2,1)S(1)} %collective-permute-done.6.refs_4_.refs_2_), custom_call_target="tpu_custom_call" | custom-call | flops 1 | bytes 1 | tf_op jit(solution)/shard_map/attend_last_cross/pallas_call | solution.py:369
  56.1 2.4 %collective-permute-start.8 = (bf16[2080,128]{1,0:T(8,128)(2,1)S(1)}, bf16[2080,128]{1,0:T(8,128)(2,1)S(1)}, u32[]{:S(2)}, u32[]{:S(2)}) collective-permute-start(bf16[2080,128]{1,0:T(8,128)(2,1)S(1)} %attend_last_cross.1), channel_id=1, source_target_pairs={{0,8},{8,0},{16,24},{24,16},{32,40},{40,32},{48,56},{56,48},{64,72... | collective-permute-start | bytes 1597448 | tf_op jit(solution)/shard_map/ppermute | solution.py:297
  58.6 0.0 copy-done.1
  58.6 5.6 %attend_own.1.own = f32[2048,256]{1,0:T(8,128)S(1)} custom-call(s32[140]{0:T(256)S(1)} %concatenate.8.info, bf16[2064,128]{1,0:T(8,128)(2,1)S(1)} %copy-done.1, f32[2048,256]{1,0:T(8,128)S(1)} %attend_near.1.refs_1_, bf16[1024,128]{1,0:T(8,128)(2,1)S(1)} %hold_shards.1.refs_2_, bf16[1024,128]{1,0:T(8,128)(2,1)S(1)} %collective-permute-done.5.refs_3_, ...), custom_call_target="tpu_custom_call" | custom-call | flops 1 | bytes 1 | tf_op jit(solution)/shard_map/attend_own/pallas_call | solution.py:369
  64.2 7.7 %collective-permute-done.8.refs_0_ = bf16[2080,128]{1,0:T(8,128)(2,1)S(1)} collective-permute-done((bf16[2080,128]{1,0:T(8,128)(2,1)S(1)}, bf16[2080,128]{1,0:T(8,128)(2,1)S(1)}, u32[]{:S(2)}, u32[]{:S(2)}) %collective-permute-start.8) | collective-permute-done | bytes 532512 | tf_op jit(solution)/shard_map/ppermute | solution.py:297
  71.9 1.2 %finish.1 = bf16[256,1024]{1,0:T(8,128)(2,1)} custom-call(f32[2048,256]{1,0:T(8,128)S(1)} %attend_own.1.own, bf16[2080,128]{1,0:T(8,128)(2,1)S(1)} %collective-permute-done.8.refs_0_), custom_call_target="tpu_custom_call" | custom-call | flops 1 | bytes 1 | tf_op jit(solution)/shard_map/finish/pallas_call | solution.py:460
  (1 shorter events, 0.0 us)
Async XLA Ops:
  1.9 12.7 %collective-permute-start.1 = (bf16[512,128]{1,0:T(8,128)(2,1)}, bf16[512,128]{1,0:T(8,128)(2,1)S(1)}, u32[]{:S(2)}, u32[]{:S(2)}) collective-permute-start(bf16[512,128]{1,0:T(8,128)(2,1)} %get-tuple-element.16.refs_1_.own), channel_id=1, source_target_pairs={{0,64},{8,72},{16,80},{24,88},{32,96},{40,104},{48,112},{56,120},{... | collective-permute-start | bytes 393224 | tf_op jit(solution)/shard_map/ppermute | solution.py:294
  2.6 15.9 %collective-permute-start = (bf16[512,128]{1,0:T(8,128)(2,1)}, bf16[512,128]{1,0:T(8,128)(2,1)S(1)}, u32[]{:S(2)}, u32[]{:S(2)}) collective-permute-start(bf16[512,128]{1,0:T(8,128)(2,1)} %get-tuple-element.16.refs_1_.own), channel_id=1, source_target_pairs={{0,192},{8,200},{16,208},{24,216},{32,224},{40,232},{48,240},{56,2... | collective-permute-start | bytes 393224 | tf_op jit(solution)/shard_map/ppermute | solution.py:294
  3.9 21.8 %collective-permute-start.4 = (bf16[512,128]{1,0:T(8,128)(2,1)}, bf16[512,128]{1,0:T(8,128)(2,1)S(1)}, u32[]{:S(2)}, u32[]{:S(2)}) collective-permute-start(bf16[512,128]{1,0:T(8,128)(2,1)} %get-tuple-element.16.refs_1_.own), channel_id=1, source_target_pairs={{128,144},{136,152},{144,160},{152,168},{160,176},{168,184},{176,1... | collective-permute-start | bytes 393224 | tf_op jit(solution)/shard_map/ppermute | solution.py:294
  10.1 15.6 %collective-permute-start.3 = (bf16[2064,128]{1,0:T(8,128)(2,1)}, bf16[2064,128]{1,0:T(8,128)(2,1)S(1)}, u32[]{:S(2)}, u32[]{:S(2)}) collective-permute-start(bf16[2064,128]{1,0:T(8,128)(2,1)} %rotate_queries.1.refs_0_), channel_id=1, source_target_pairs={{0,8},{8,0},{16,24},{24,16},{32,40},{40,32},{48,56},{56,48},{64,72... | collective-permute-start | bytes 1585160 | tf_op jit(solution)/shard_map/ppermute | solution.py:297
  14.7 1.0 %copy-start = (bf16[2064,128]{1,0:T(8,128)(2,1)S(1)}, bf16[2064,128]{1,0:T(8,128)(2,1)}, u32[]{:S(2)}) copy-start(bf16[2064,128]{1,0:T(8,128)(2,1)} %rotate_queries.1.refs_0_) | copy-start | bytes 1585156
  15.7 0.9 %copy-start.2 = (bf16[512,128]{1,0:T(8,128)(2,1)S(1)}, bf16[512,128]{1,0:T(8,128)(2,1)}, u32[]{:S(2)}) copy-start(bf16[512,128]{1,0:T(8,128)(2,1)} %get-tuple-element.16.refs_1_.own) | copy-start | bytes 393220
  18.5 7.3 %copy-start.3 = (bf16[512,128]{1,0:T(8,128)(2,1)S(1)}, bf16[512,128]{1,0:T(8,128)(2,1)}, u32[]{:S(2)}) copy-start(bf16[512,128]{1,0:T(8,128)(2,1)} %get-tuple-element.16.refs_1_.own) | copy-start | bytes 393220
  19.1 10.8 %collective-permute-start.2 = (bf16[512,128]{1,0:T(8,128)(2,1)S(1)}, bf16[512,128]{1,0:T(8,128)(2,1)S(1)}, u32[]{:S(2)}, u32[]{:S(2)}) collective-permute-start(bf16[512,128]{1,0:T(8,128)(2,1)S(1)} %choose_shard.1.opposite), channel_id=1, source_target_pairs={{0,192},{8,200},{32,224},{40,232},{80,144},{88,152},{112,176},{120... | collective-permute-start | bytes 393224 | tf_op jit(solution)/shard_map/ppermute | solution.py:294
  30.5 17.5 %collective-permute-start.5 = (bf16[1024,128]{1,0:T(8,128)(2,1)S(1)}, bf16[1024,128]{1,0:T(8,128)(2,1)S(1)}, u32[]{:S(2)}, u32[]{:S(2)}) collective-permute-start(bf16[1024,128]{1,0:T(8,128)(2,1)S(1)} %hold_shards.1.refs_2_), channel_id=1, source_target_pairs={{0,16},{8,24},{16,32},{24,40},{32,48},{40,56},{48,64},{56,72},{64,... | collective-permute-start | bytes 786440 | tf_op jit(solution)/shard_map/ppermute | solution.py:294
  36.8 13.3 %collective-permute-start.7 = (bf16[1024,128]{1,0:T(8,128)(2,1)S(1)}, bf16[1024,128]{1,0:T(8,128)(2,1)S(1)}, u32[]{:S(2)}, u32[]{:S(2)}) collective-permute-start(bf16[1024,128]{1,0:T(8,128)(2,1)S(1)} %hold_shards.1.refs_2_), channel_id=1, source_target_pairs={{0,224},{8,232},{16,48},{24,56},{48,80},{56,88},{64,32},{72,40},{8... | collective-permute-start | bytes 786440 | tf_op jit(solution)/shard_map/ppermute | solution.py:294
  39.4 14.5 %collective-permute-start.6 = (bf16[1024,128]{1,0:T(8,128)(2,1)S(1)}, bf16[1024,128]{1,0:T(8,128)(2,1)S(1)}, u32[]{:S(2)}, u32[]{:S(2)}) collective-permute-start(bf16[1024,128]{1,0:T(8,128)(2,1)S(1)} %hold_shards.1.refs_2_), channel_id=1, source_target_pairs={{0,240},{8,248},{64,48},{72,56},{80,64},{88,72},{96,80},{104,88},{... | collective-permute-start | bytes 786440 | tf_op jit(solution)/shard_map/ppermute | solution.py:294
  53.4 5.2 %copy-start.1 = (bf16[2064,128]{1,0:T(8,128)(2,1)S(1)}, bf16[2064,128]{1,0:T(8,128)(2,1)}, u32[]{:S(2)}) copy-start(bf16[2064,128]{1,0:T(8,128)(2,1)} %rotate_queries.1.refs_0_) | copy-start | bytes 1585156
  56.1 15.7 %collective-permute-start.8 = (bf16[2080,128]{1,0:T(8,128)(2,1)S(1)}, bf16[2080,128]{1,0:T(8,128)(2,1)S(1)}, u32[]{:S(2)}, u32[]{:S(2)}) collective-permute-start(bf16[2080,128]{1,0:T(8,128)(2,1)S(1)} %attend_last_cross.1), channel_id=1, source_target_pairs={{0,8},{8,0},{16,24},{24,16},{32,40},{40,32},{48,56},{56,48},{64,72... | collective-permute-start | bytes 1597448 | tf_op jit(solution)/shard_map/ppermute | solution.py:297

commit v4 on v3

--- a/solution.py
+++ b/solution.py
@@ -178,7 +178,7 @@
             seen = [block(number, a, b) > 0 for a in range(2) for b in range(2)]
             any_seen = seen[0] | seen[1] | seen[2] | seen[3]
             if near:
-                late.append((shard, number, any_seen & (number * rows >= prompt)))
+                late.append((shard, number, any_seen))
             else:
                 all_seen = seen[0] & seen[1] & seen[2] & seen[3]
                 all_seen = all_seen & (number < mine) & (number * rows < prompt)
@@ -323,7 +323,9 @@
     inside = move(
         kv, lambda z: z + half if z < half else (z - half if z < period and z % 2 == 0 else None)
     )
-    beneath = move(kv, lambda z: z + 1 if period <= z < depth - 1 else None)
+    beneath = move(
+        kv, lambda z: 2 if z == 0 else (z + 1 if period <= z < depth - 1 else None)
+    )
 
     query = pl.pallas_call(
         query_kernel,
@@ -347,10 +349,16 @@
     def number(offset):
         return (plane + offset) % period * 2 + lane
 
-    odd = plane % 2
-    numbers = [mine, mine + 1 - 2 * lane, mine, mine - 2]
+    turned = ((plane % 2 == 1) | (plane == half + 2)).astype(jnp.int32)
+    never = ring - 1
+    second_near = jnp.where(plane == 2, lane, jnp.where(plane > period, mine - 2, never))
+
+    def aslant(offset):
+        return jnp.where(plane == 2, never, number(offset))
+
+    numbers = [mine, mine + 1 - 2 * lane, jnp.where(plane < period, never, mine), second_near]
     numbers += [number(0), number(4), number(-1), number(3), number(1), number(5)]
-    numbers += [number(2 + 4 * odd), number(6 - 4 * odd)]
+    numbers += [aslant(2 + 4 * turned), aslant(6 - 4 * turned)]
     numbers = jnp.stack(numbers).astype(jnp.int32)
     info_own = jnp.concatenate([numbers, block_mask.reshape(-1)])
     mask_cross = query_cross[heads * rows, :].astype(jnp.int32)
@@ -422,9 +430,10 @@
     )(numbers, kv, first, second)
     low = move(held, lambda z: z + 1 if z + 1 < depth else None)
     high = move(held, lambda z: z - 1 if not 1 <= z < half else None)
-    skip = move(
-        held, lambda z: None if z in (2, depth - 1) else (z + 2 if z % 2 else z - 2)
-    )
+    steps = {z: z + 2 if z % 2 or z == half else z - 2 for z in range(depth)}
+    for unused in (2, period, depth - 1):
+        del steps[unused]
+    skip = move(held, steps.get)
 
     held_slots = [(HELD, False), (HELD + 1, False)]
     low_slots = [(LOW, False), (LOW + 1, False)]
@@ -436,15 +445,15 @@
     (cross,) = attend(
         info,
         [job(1, True)],
-        skip_slots + low_slots,
+        high_slots + low_slots,
         [query_cross],
         [cross],
-        [skip, low],
+        [high, low],
         [2, 2],
         "attend_next_cross",
     )
     (cross,) = attend(
-        info, [job(1, True, True)], high_slots, [query_cross], [cross], [high], [2], "attend_last_cross"
+        info, [job(1, True, True)], skip_slots, [query_cross], [cross], [skip], [2], "attend_last_cross"
     )
     other = swap(cross)
     (own,) = attend(

time: 73.5 us -> 74 us (level)
  the two profiles are of different devices: /device:TPU:326 before, /device:TPU:224 now
where the time goes in v4:
time: 74 us; the launch traced here: 73.5 us
  starting transfers between devices  29.7 us (40%)
  Pallas kernels  26.5 us (36%)
  waiting for transfers between devices  14 us (19%)
  local copies, waits for them, and re-layouts  2.99 us (4%)
    ppermute x7, starting transfers between devices, move(): return lax.ppermute(array, 'ctx', pairs)  24 us
    pallas_call x6, Pallas kernels, attend(): pl.pallas_call(functools.partial(attend_kernel, jobs=jobs, slots=slots, c...  19 us
    ppermute x7, waiting for transfers between devices, move(): return lax.ppermute(array, 'ctx', pairs)  11.4 us
    ppermute x2, starting transfers between devices, swap(): return lax.ppermute(array, 'ctx', [(c, c ^ 1) for c in range(ring)])  5.71 us
    pallas_call x1, Pallas kernels, local(): pl.pallas_call(query_kernel, out_shape=shape((heads * rows + PAD, HEAD),...  3.21 us
    ppermute x2, waiting for transfers between devices, swap(): return lax.ppermute(array, 'ctx', [(c, c ^ 1) for c in range(ring)])  2.67 us
    unnamed x8, local copies, waits for them, and re-layouts  1.96 us
    pallas_call x1, Pallas kernels, local(): pl.pallas_call(key_kernel, out_shape=[shape((2 * rows, HEAD), jnp.bfloat1...  1.93 us
  transfers between devices with their start and end apart: 9, of which 6 were waited for; matrix products, arithmetic and copies ran while one was open for 1% of the time, Pallas kernels for 28%

profile of v4, /device:TPU:224, one launch (start us, length us, event | category | flops | bytes accessed | tf_op | source)
XLA Modules:
  0.0 73.5 jit_solution(16572073459634473038)
XLA Ops:
  0.0 1.9 %rotate_keys.1 = (bf16[512,128]{1,0:T(8,128)(2,1)}, f32[256,128]{1,0:T(8,128)}, f32[256,128]{1,0:T(8,128)}) custom-call(bf16[256,128]{1,0:T(8,128)(2,1)} %keys.1, bf16[256,128]{1,0:T(8,128)(2,1)} %values.1, f32[1,128]{1,0:T(1,128)} %bitcast.22, s32[1,256]{1,0:T(1,128)} %bitcast.20, f32[1,128]{1,0:T(1,128)} %constant.89.clone.freq), custom_call_target="tpu_custom_call" | custom-call | flops 1 | bytes 1 | tf_op jit(solution)/shard_map/rotate_keys/pallas_call | solution.py:301
  1.9 1.3 %collective-permute-start.1 = (bf16[512,128]{1,0:T(8,128)(2,1)}, bf16[512,128]{1,0:T(8,128)(2,1)S(1)}, u32[]{:S(2)}, u32[]{:S(2)}) collective-permute-start(bf16[512,128]{1,0:T(8,128)(2,1)} %get-tuple-element.16.refs_1_.own), channel_id=1, source_target_pairs={{0,64},{8,72},{16,80},{24,88},{32,96},{40,104},{48,112},{56,120},{... | collective-permute-start | bytes 393224 | tf_op jit(solution)/shard_map/ppermute | solution.py:294
  3.2 5.8 %collective-permute-start = (bf16[512,128]{1,0:T(8,128)(2,1)}, bf16[512,128]{1,0:T(8,128)(2,1)S(1)}, u32[]{:S(2)}, u32[]{:S(2)}) collective-permute-start(bf16[512,128]{1,0:T(8,128)(2,1)} %get-tuple-element.16.refs_1_.own), channel_id=1, source_target_pairs={{0,192},{8,200},{16,208},{24,216},{32,224},{40,232},{48,240},{56,2... | collective-permute-start | bytes 393224 | tf_op jit(solution)/shard_map/ppermute | solution.py:294
  9.0 0.7 collective-permute-start.4
  9.7 3.2 %rotate_queries.1.refs_0_ = bf16[2064,128]{1,0:T(8,128)(2,1)} custom-call(bf16[256,1024]{1,0:T(8,128)(2,1)} %queries.1, f32[1,128]{1,0:T(1,128)} %bitcast.23, f32[256,128]{1,0:T(8,128)} %get-tuple-element.14.cosine, f32[256,128]{1,0:T(8,128)} %get-tuple-element.15.sine, s32[2,64]{1,0:T(2,128)} %mask.1, s32[1,256]{1,0:T(1,128)} %bitcast.21), custom_call_target="tpu_custom_call" | custom-call | flops 1 | bytes 1 | tf_op jit(solution)/shard_map/rotate_queries/pallas_call | solution.py:330
  12.9 3.5 %collective-permute-start.3 = (bf16[2064,128]{1,0:T(8,128)(2,1)}, bf16[2064,128]{1,0:T(8,128)(2,1)S(1)}, u32[]{:S(2)}, u32[]{:S(2)}) collective-permute-start(bf16[2064,128]{1,0:T(8,128)(2,1)} %rotate_queries.1.refs_0_), channel_id=1, source_target_pairs={{0,8},{8,0},{16,24},{24,16},{32,40},{40,32},{48,56},{56,48},{64,72... | collective-permute-start | bytes 1585160 | tf_op jit(solution)/shard_map/ppermute | solution.py:297
  16.6 0.8 %reshape.5 = s32[128]{0:T(128)S(1)} reshape(s32[2,64]{1,0:T(2,128)} %mask.1) | data formatting | bytes 1024 | tf_op jit(solution)/shard_map/reshape | solution.py:363
  17.3 0.1 stack.51.info
  17.4 0.1 concatenate.8.info
  17.5 2.8 %collective-permute-done.1.inside = bf16[512,128]{1,0:T(8,128)(2,1)S(1)} collective-permute-done((bf16[512,128]{1,0:T(8,128)(2,1)}, bf16[512,128]{1,0:T(8,128)(2,1)S(1)}, u32[]{:S(2)}, u32[]{:S(2)}) %collective-permute-start.1) | collective-permute-done | bytes 131104 | tf_op jit(solution)/shard_map/ppermute | solution.py:294
  20.4 0.0 copy-start
  20.4 1.0 %copy-done = bf16[2064,128]{1,0:T(8,128)(2,1)S(1)} copy-done((bf16[2064,128]{1,0:T(8,128)(2,1)S(1)}, bf16[2064,128]{1,0:T(8,128)(2,1)}, u32[]{:S(2)}) %copy-start) | copy-done | bytes 528408
  21.4 0.0 copy-start.2
  21.4 0.9 %copy-done.2 = bf16[512,128]{1,0:T(8,128)(2,1)S(1)} copy-done((bf16[512,128]{1,0:T(8,128)(2,1)S(1)}, bf16[512,128]{1,0:T(8,128)(2,1)}, u32[]{:S(2)}) %copy-start.2) | copy-done | bytes 131096
  22.3 0.7 attend_near.1.refs_1_
  23.0 0.0 copy-start.3
  23.0 0.0 collective-permute-done.across
  23.0 0.6 choose_shard.1.opposite
  23.6 3.7 %collective-permute-start.2 = (bf16[512,128]{1,0:T(8,128)(2,1)S(1)}, bf16[512,128]{1,0:T(8,128)(2,1)S(1)}, u32[]{:S(2)}, u32[]{:S(2)}) collective-permute-start(bf16[512,128]{1,0:T(8,128)(2,1)S(1)} %choose_shard.1.opposite), channel_id=1, source_target_pairs={{0,192},{8,200},{32,224},{40,232},{80,144},{88,152},{112,176},{120... | collective-permute-start | bytes 393224 | tf_op jit(solution)/shard_map/ppermute | solution.py:294
  27.3 1.2 %collective-permute-done.3.refs_0_ = bf16[2064,128]{1,0:T(8,128)(2,1)S(1)} collective-permute-done((bf16[2064,128]{1,0:T(8,128)(2,1)}, bf16[2064,128]{1,0:T(8,128)(2,1)S(1)}, u32[]{:S(2)}, u32[]{:S(2)}) %collective-permute-start.3) | collective-permute-done | bytes 528416 | tf_op jit(solution)/shard_map/ppermute | solution.py:297
  28.5 0.1 concatenate.9.info
  28.6 0.0 collective-permute-done.4.refs_2_.refs_6_
  28.6 0.0 copy-done.3
  28.6 0.7 attend_near_cross.1.refs_1_
  29.3 2.0 %collective-permute-done.2.second = bf16[512,128]{1,0:T(8,128)(2,1)S(1)} collective-permute-done((bf16[512,128]{1,0:T(8,128)(2,1)S(1)}, bf16[512,128]{1,0:T(8,128)(2,1)S(1)}, u32[]{:S(2)}, u32[]{:S(2)}) %collective-permute-start.2) | collective-permute-done | bytes 131104 | tf_op jit(solution)/shard_map/ppermute | solution.py:294
  31.4 0.6 hold_shards.1.refs_2_
  32.0 7.2 %collective-permute-start.5 = (bf16[1024,128]{1,0:T(8,128)(2,1)S(1)}, bf16[1024,128]{1,0:T(8,128)(2,1)S(1)}, u32[]{:S(2)}, u32[]{:S(2)}) collective-permute-start(bf16[1024,128]{1,0:T(8,128)(2,1)S(1)} %hold_shards.1.refs_2_), channel_id=1, source_target_pairs={{0,16},{8,24},{16,32},{24,40},{32,48},{40,56},{48,64},{56,72},{64,... | collective-permute-start | bytes 786440 | tf_op jit(solution)/shard_map/ppermute | solution.py:294
  39.2 1.9 %collective-permute-start.6 = (bf16[1024,128]{1,0:T(8,128)(2,1)S(1)}, bf16[1024,128]{1,0:T(8,128)(2,1)S(1)}, u32[]{:S(2)}, u32[]{:S(2)}) collective-permute-start(bf16[1024,128]{1,0:T(8,128)(2,1)S(1)} %hold_shards.1.refs_2_), channel_id=1, source_target_pairs={{0,240},{8,248},{64,48},{72,56},{80,64},{88,72},{96,80},{104,88},{... | collective-permute-start | bytes 786440 | tf_op jit(solution)/shard_map/ppermute | solution.py:294
  41.1 3.4 %collective-permute-start.7 = (bf16[1024,128]{1,0:T(8,128)(2,1)S(1)}, bf16[1024,128]{1,0:T(8,128)(2,1)S(1)}, u32[]{:S(2)}, u32[]{:S(2)}) collective-permute-start(bf16[1024,128]{1,0:T(8,128)(2,1)S(1)} %hold_shards.1.refs_2_), channel_id=1, source_target_pairs={{0,224},{8,232},{16,48},{24,56},{48,80},{56,88},{64,96},{72,104},{... | collective-permute-start | bytes 786440 | tf_op jit(solution)/shard_map/ppermute | solution.py:294
  44.5 2.0 %attend_held_cross.1.refs_1_ = f32[2048,256]{1,0:T(8,128)S(1)} custom-call(s32[268]{0:T(512)S(1)} %concatenate.9.info, bf16[2064,128]{1,0:T(8,128)(2,1)S(1)} %collective-permute-done.3.refs_0_, f32[2048,256]{1,0:T(8,128)S(1)} %attend_near_cross.1.refs_1_, bf16[1024,128]{1,0:T(8,128)(2,1)S(1)} %hold_shards.1.refs_2_), custom_call_target="tpu_custom_call" | custom-call | flops 1 | bytes 1 | tf_op jit(solution)/shard_map/attend_held_cross/pallas_call | solution.py:377
  46.5 0.0 collective-permute-done.5.refs_3_
  46.5 2.6 %collective-permute-done.6.refs_4_.refs_2_ = bf16[1024,128]{1,0:T(8,128)(2,1)S(1)} collective-permute-done((bf16[1024,128]{1,0:T(8,128)(2,1)S(1)}, bf16[1024,128]{1,0:T(8,128)(2,1)S(1)}, u32[]{:S(2)}, u32[]{:S(2)}) %collective-permute-start.6) | collective-permute-done | bytes 262176 | tf_op jit(solution)/shard_map/ppermute | solution.py:294
  49.1 3.3 %attend_next_cross.1.refs_1_ = f32[2048,256]{1,0:T(8,128)S(1)} custom-call(s32[268]{0:T(512)S(1)} %concatenate.9.info, bf16[2064,128]{1,0:T(8,128)(2,1)S(1)} %collective-permute-done.3.refs_0_, f32[2048,256]{1,0:T(8,128)S(1)} %attend_held_cross.1.refs_1_, bf16[1024,128]{1,0:T(8,128)(2,1)S(1)} %collective-permute-done.6.refs_4_.refs_2_, ...), custom_call_target="tpu_custom_call" | custom-call | flops 1 | bytes 1 | tf_op jit(solution)/shard_map/attend_next_cross/pallas_call | solution.py:377
  52.4 0.0 copy-start.1
  52.4 3.8 %collective-permute-done.7.refs_5_.refs_2_ = bf16[1024,128]{1,0:T(8,128)(2,1)S(1)} collective-permute-done((bf16[1024,128]{1,0:T(8,128)(2,1)S(1)}, bf16[1024,128]{1,0:T(8,128)(2,1)S(1)}, u32[]{:S(2)}, u32[]{:S(2)}) %collective-permute-start.7) | collective-permute-done | bytes 262176 | tf_op jit(solution)/shard_map/ppermute | solution.py:294
  56.3 2.2 %attend_last_cross.1 = bf16[2080,128]{1,0:T(8,128)(2,1)S(1)} custom-call(s32[268]{0:T(512)S(1)} %concatenate.9.info, bf16[2064,128]{1,0:T(8,128)(2,1)S(1)} %collective-permute-done.3.refs_0_, f32[2048,256]{1,0:T(8,128)S(1)} %attend_next_cross.1.refs_1_, bf16[1024,128]{1,0:T(8,128)(2,1)S(1)} %collective-permute-done.7.refs_5_.refs_2_), custom_call_target="tpu_custom_call" | custom-call | flops 1 | bytes 1 | tf_op jit(solution)/shard_map/attend_last_cross/pallas_call | solution.py:377
  58.4 2.2 %collective-permute-start.8 = (bf16[2080,128]{1,0:T(8,128)(2,1)S(1)}, bf16[2080,128]{1,0:T(8,128)(2,1)S(1)}, u32[]{:S(2)}, u32[]{:S(2)}) collective-permute-start(bf16[2080,128]{1,0:T(8,128)(2,1)S(1)} %attend_last_cross.1), channel_id=1, source_target_pairs={{0,8},{8,0},{16,24},{24,16},{32,40},{40,32},{48,56},{56,48},{64,72... | collective-permute-start | bytes 1597448 | tf_op jit(solution)/shard_map/ppermute | solution.py:297
  60.7 0.0 copy-done.1
  60.7 10.2 %attend_own.1.own = f32[2048,256]{1,0:T(8,128)S(1)} custom-call(s32[140]{0:T(256)S(1)} %concatenate.8.info, bf16[2064,128]{1,0:T(8,128)(2,1)S(1)} %copy-done.1, f32[2048,256]{1,0:T(8,128)S(1)} %attend_near.1.refs_1_, bf16[1024,128]{1,0:T(8,128)(2,1)S(1)} %hold_shards.1.refs_2_, bf16[1024,128]{1,0:T(8,128)(2,1)S(1)} %collective-permute-done.5.refs_3_, ...), custom_call_target="tpu_custom_call" | custom-call | flops 1 | bytes 1 | tf_op jit(solution)/shard_map/attend_own/pallas_call | solution.py:377
  70.9 1.5 %collective-permute-done.8.refs_0_ = bf16[2080,128]{1,0:T(8,128)(2,1)S(1)} collective-permute-done((bf16[2080,128]{1,0:T(8,128)(2,1)S(1)}, bf16[2080,128]{1,0:T(8,128)(2,1)S(1)}, u32[]{:S(2)}, u32[]{:S(2)}) %collective-permute-start.8) | collective-permute-done | bytes 532512 | tf_op jit(solution)/shard_map/ppermute | solution.py:297
  72.3 1.2 %finish.1 = bf16[256,1024]{1,0:T(8,128)(2,1)} custom-call(f32[2048,256]{1,0:T(8,128)S(1)} %attend_own.1.own, bf16[2080,128]{1,0:T(8,128)(2,1)S(1)} %collective-permute-done.8.refs_0_), custom_call_target="tpu_custom_call" | custom-call | flops 1 | bytes 1 | tf_op jit(solution)/shard_map/finish/pallas_call | solution.py:469
  (1 shorter events, 0.0 us)
Async XLA Ops:
  1.9 18.4 %collective-permute-start.1 = (bf16[512,128]{1,0:T(8,128)(2,1)}, bf16[512,128]{1,0:T(8,128)(2,1)S(1)}, u32[]{:S(2)}, u32[]{:S(2)}) collective-permute-start(bf16[512,128]{1,0:T(8,128)(2,1)} %get-tuple-element.16.refs_1_.own), channel_id=1, source_target_pairs={{0,64},{8,72},{16,80},{24,88},{32,96},{40,104},{48,112},{56,120},{... | collective-permute-start | bytes 393224 | tf_op jit(solution)/shard_map/ppermute | solution.py:294
  3.2 19.8 %collective-permute-start = (bf16[512,128]{1,0:T(8,128)(2,1)}, bf16[512,128]{1,0:T(8,128)(2,1)S(1)}, u32[]{:S(2)}, u32[]{:S(2)}) collective-permute-start(bf16[512,128]{1,0:T(8,128)(2,1)} %get-tuple-element.16.refs_1_.own), channel_id=1, source_target_pairs={{0,192},{8,200},{16,208},{24,216},{32,224},{40,232},{48,240},{56,2... | collective-permute-start | bytes 393224 | tf_op jit(solution)/shard_map/ppermute | solution.py:294
  9.0 19.6 %collective-permute-start.4 = (bf16[512,128]{1,0:T(8,128)(2,1)}, bf16[512,128]{1,0:T(8,128)(2,1)S(1)}, u32[]{:S(2)}, u32[]{:S(2)}) collective-permute-start(bf16[512,128]{1,0:T(8,128)(2,1)} %get-tuple-element.16.refs_1_.own), channel_id=1, source_target_pairs={{0,32},{8,40},{128,144},{136,152},{144,160},{152,168},{160,176},{1... | collective-permute-start | bytes 393224 | tf_op jit(solution)/shard_map/ppermute | solution.py:294
  12.9 15.6 %collective-permute-start.3 = (bf16[2064,128]{1,0:T(8,128)(2,1)}, bf16[2064,128]{1,0:T(8,128)(2,1)S(1)}, u32[]{:S(2)}, u32[]{:S(2)}) collective-permute-start(bf16[2064,128]{1,0:T(8,128)(2,1)} %rotate_queries.1.refs_0_), channel_id=1, source_target_pairs={{0,8},{8,0},{16,24},{24,16},{32,40},{40,32},{48,56},{56,48},{64,72... | collective-permute-start | bytes 1585160 | tf_op jit(solution)/shard_map/ppermute | solution.py:297
  20.4 1.0 %copy-start = (bf16[2064,128]{1,0:T(8,128)(2,1)S(1)}, bf16[2064,128]{1,0:T(8,128)(2,1)}, u32[]{:S(2)}) copy-start(bf16[2064,128]{1,0:T(8,128)(2,1)} %rotate_queries.1.refs_0_) | copy-start | bytes 1585156
  21.4 0.9 %copy-start.2 = (bf16[512,128]{1,0:T(8,128)(2,1)S(1)}, bf16[512,128]{1,0:T(8,128)(2,1)}, u32[]{:S(2)}) copy-start(bf16[512,128]{1,0:T(8,128)(2,1)} %get-tuple-element.16.refs_1_.own) | copy-start | bytes 393220
  23.0 5.6 %copy-start.3 = (bf16[512,128]{1,0:T(8,128)(2,1)S(1)}, bf16[512,128]{1,0:T(8,128)(2,1)}, u32[]{:S(2)}) copy-start(bf16[512,128]{1,0:T(8,128)(2,1)} %get-tuple-element.16.refs_1_.own) | copy-start | bytes 393220
  23.6 7.8 %collective-permute-start.2 = (bf16[512,128]{1,0:T(8,128)(2,1)S(1)}, bf16[512,128]{1,0:T(8,128)(2,1)S(1)}, u32[]{:S(2)}, u32[]{:S(2)}) collective-permute-start(bf16[512,128]{1,0:T(8,128)(2,1)S(1)} %choose_shard.1.opposite), channel_id=1, source_target_pairs={{0,192},{8,200},{32,224},{40,232},{80,144},{88,152},{112,176},{120... | collective-permute-start | bytes 393224 | tf_op jit(solution)/shard_map/ppermute | solution.py:294
  32.0 14.5 %collective-permute-start.5 = (bf16[1024,128]{1,0:T(8,128)(2,1)S(1)}, bf16[1024,128]{1,0:T(8,128)(2,1)S(1)}, u32[]{:S(2)}, u32[]{:S(2)}) collective-permute-start(bf16[1024,128]{1,0:T(8,128)(2,1)S(1)} %hold_shards.1.refs_2_), channel_id=1, source_target_pairs={{0,16},{8,24},{16,32},{24,40},{32,48},{40,56},{48,64},{56,72},{64,... | collective-permute-start | bytes 786440 | tf_op jit(solution)/shard_map/ppermute | solution.py:294
  39.2 9.9 %collective-permute-start.6 = (bf16[1024,128]{1,0:T(8,128)(2,1)S(1)}, bf16[1024,128]{1,0:T(8,128)(2,1)S(1)}, u32[]{:S(2)}, u32[]{:S(2)}) collective-permute-start(bf16[1024,128]{1,0:T(8,128)(2,1)S(1)} %hold_shards.1.refs_2_), channel_id=1, source_target_pairs={{0,240},{8,248},{64,48},{72,56},{80,64},{88,72},{96,80},{104,88},{... | collective-permute-start | bytes 786440 | tf_op jit(solution)/shard_map/ppermute | solution.py:294
  41.1 15.1 %collective-permute-start.7 = (bf16[1024,128]{1,0:T(8,128)(2,1)S(1)}, bf16[1024,128]{1,0:T(8,128)(2,1)S(1)}, u32[]{:S(2)}, u32[]{:S(2)}) collective-permute-start(bf16[1024,128]{1,0:T(8,128)(2,1)S(1)} %hold_shards.1.refs_2_), channel_id=1, source_target_pairs={{0,224},{8,232},{16,48},{24,56},{48,80},{56,88},{64,96},{72,104},{... | collective-permute-start | bytes 786440 | tf_op jit(solution)/shard_map/ppermute | solution.py:294
  52.4 8.3 %copy-start.1 = (bf16[2064,128]{1,0:T(8,128)(2,1)S(1)}, bf16[2064,128]{1,0:T(8,128)(2,1)}, u32[]{:S(2)}) copy-start(bf16[2064,128]{1,0:T(8,128)(2,1)} %rotate_queries.1.refs_0_) | copy-start | bytes 1585156
  58.4 13.9 %collective-permute-start.8 = (bf16[2080,128]{1,0:T(8,128)(2,1)S(1)}, bf16[2080,128]{1,0:T(8,128)(2,1)S(1)}, u32[]{:S(2)}, u32[]{:S(2)}) collective-permute-start(bf16[2080,128]{1,0:T(8,128)(2,1)S(1)} %attend_last_cross.1), channel_id=1, source_target_pairs={{0,8},{8,0},{16,24},{24,16},{32,40},{40,32},{48,56},{56,48},{64,72... | collective-permute-start | bytes 1597448 | tf_op jit(solution)/shard_map/ppermute | solution.py:297
